TPU v7x, 128 devices: a whole 4x4x4 slice. The times are simulated.
128 devices in a mesh: ctx: 16 (over z_lo, y, core), resp: 8 (over x, z_hi).
Axes of the slice: x: 4, y: 4, z: 4 (z_hi: 2, z_lo: 2; z = z_hi * 2 + z_lo), core: 2. Of those that a mesh axis runs over, the one named last changes fastest.
Arguments:
- queries: bfloat16 [8, 512, 36864], P('resp', None, 'ctx'), may hold values from -6 to 6
- attn_cot: bfloat16 [8, 512, 32768], P('resp', None, 'ctx'), may hold values from -24 to 24
- prompt_latent: bfloat16 [1024, 576], P('ctx'), may hold values from -6 to 6
- response_latent: bfloat16 [8, 512, 576], P('resp'), may hold values from -6 to 6
- log_ratio: float32 [8, 512], P('resp'), may hold values from -0.6 to 0.6
- lengths: int32 [8, 2], P('resp'), may hold values from 64 to 256, as said below
- chosen: int32 [8], P('resp'), may hold values from 0 to 1
- moe_cot: bfloat16 [8, 512, 7168], P('resp', 'ctx'), may hold values from -24 to 24
- expert_ids: int32 [8, 512, 8], P('resp', 'ctx'), may hold values from 0 to 255, all different within a row; in each aligned block of 32 rows (0 to 31, 32 to 63, ..., all dimensions but the last counted through in order) at most 2 rows name the same one
- router_logits: float32 [8, 512, 8], P('resp', 'ctx'), may hold values from -6 to 6
- expert_outputs: bfloat16 [128, 256, 2, 7168], P(None, ('ctx', 'resp')), may hold values from -0.1796875 to 0.1796875
Outputs:
- grad_query: bfloat16 [8, 512, 36864], P('resp', None, 'ctx')
- grad_prompt: float32 [1024, 576], P(('ctx', 'resp'))
- grad_response: float32 [8, 512, 576], P('resp', 'ctx')
- expert_row_grads: bfloat16 [128, 256, 2, 7168], P(None, ('ctx', 'resp'))
- grad_router: float32 [8, 512, 8], P('resp', 'ctx')
Inputs may be any that keep to these rules, and one draw needn't show every extreme that they name: `lengths`: every draw has a response of length 256 and one of length 64. `expert_ids`: each row names 8 different experts; among the rows of one device no expert is named more than 2 times, and in every draw some device's rows name some expert exactly 2 times.
All inputs are finite; a program needn't handle non-finite values.
Results may differ from a plain program's by a relative error of at most 0.012.
The roundings to bfloat16 on the way count: a program that leaves them out, or rounds other values in their place, can miss the bound.
Values may be sent and summed in bfloat16 or wider, within the bound.
No kernel may reach another device: no remote copies, remote signals or barrier semaphores. Data moves between devices by JAX's collectives and lax.ppermute only.
A program may use at most 192 MiB of HBM per device.

v0:
```python
import jax
import jax.numpy as jnp
from jax import lax
from jax.sharding import PartitionSpec as P

EXPERTS = 256
CAP = 2


score_scale = 192.0 ** (-0.5)
preference_beta = 0.5
route_scale = 2.5


def pair_coefficients(log_ratio, lengths, chosen):
    pair_count = log_ratio.shape[0]
    half_rows = log_ratio.shape[1] // 2
    position = jnp.arange(half_rows, dtype=jnp.int32)
    live_mask = position[None, None, :] < lengths[:, :, None]
    ratios = log_ratio.reshape(pair_count, 2, half_rows)
    totals = jnp.sum(jnp.where(live_mask, ratios, jnp.zeros_like(ratios)), axis=2)
    margin = jnp.where(chosen == 0, totals[:, 0] - totals[:, 1], totals[:, 1] - totals[:, 0])
    weight = preference_beta * jax.nn.sigmoid(-preference_beta * margin)
    member = jnp.arange(2, dtype=jnp.int32)
    signed = jnp.where(member[None, :] == chosen[:, None], -weight[:, None], weight[:, None])
    return (signed[:, :, None] * live_mask.astype(signed.dtype)).reshape(pair_count, 2 * half_rows)


def allowed_keys(row_count, prompt_count):
    half_rows = row_count // 2
    query_index = jnp.arange(row_count, dtype=jnp.int32)[:, None]
    column_index = jnp.arange(prompt_count + row_count, dtype=jnp.int32)[None, :] - prompt_count
    same_answer = (
        (column_index >= 0)
        & (column_index // half_rows == query_index // half_rows)
        & (column_index <= query_index)
    )
    return (column_index < 0) | same_answer


def on_device(
    queries,
    attn_cot,
    prompt_latent,
    response_latent,
    log_ratio,
    lengths,
    chosen,
    moe_cot,
    expert_ids,
    router_logits,
    expert_outputs,
):
    width = prompt_latent.shape[1]
    row_count = queries.shape[1]
    head_count = queries.shape[2] // width
    rank = attn_cot.shape[2] // head_count
    coefficient = pair_coefficients(log_ratio, lengths, chosen)[0]
    gathered = lax.all_gather(prompt_latent, "ctx", axis=0, tiled=True)
    prompt_count = gathered.shape[0]
    key_rows = jnp.concatenate([gathered, response_latent[0]], axis=0)
    allowed = allowed_keys(row_count, prompt_count)
    query = queries[0].reshape(row_count, head_count, width)
    cot_heads = attn_cot[0].reshape(row_count, head_count, rank)
    scores = (
        jnp.einsum("ihc,jc->hij", query, key_rows, preferred_element_type=jnp.float32) * score_scale
    )
    scores = jnp.where(allowed[None, :, :], scores, -jnp.inf)
    row_top = jnp.max(scores, axis=2, keepdims=True)
    exponent = jnp.exp(scores - row_top)
    soft_weights = exponent / jnp.sum(exponent, axis=2, keepdims=True)
    soft_rounded = soft_weights.astype(jnp.bfloat16)
    values = key_rows[:, :rank]
    grad_out = (coefficient[:, None, None] * cot_heads.astype(jnp.float32)).astype(jnp.bfloat16)
    attn_out = jnp.einsum("hij,jc->ihc", soft_rounded, values, preferred_element_type=jnp.float32)
    row_delta = jnp.sum(grad_out.astype(jnp.float32) * attn_out, axis=2)
    prob_grad = jnp.einsum("ihc,jc->hij", grad_out, values, preferred_element_type=jnp.float32)
    score_grad = (soft_weights * (prob_grad - row_delta.T[:, :, None])).astype(jnp.bfloat16)
    grad_query = score_scale * jnp.einsum(
        "hij,jc->ihc", score_grad, key_rows, preferred_element_type=jnp.float32
    )
    grad_query = grad_query.astype(jnp.bfloat16).reshape(1, row_count, head_count * width)
    key_grad = score_scale * jnp.einsum(
        "hij,ihc->jc", score_grad, query, preferred_element_type=jnp.float32
    )
    value_grad = jnp.einsum(
        "hij,ihc->jc", soft_rounded, grad_out, preferred_element_type=jnp.float32
    )
    key_grad = key_grad + jnp.pad(value_grad, ((0, 0), (0, width - rank)))
    prompt_terms = key_grad[:prompt_count]
    grad_prompt = lax.psum_scatter(prompt_terms, ("ctx", "resp"), scatter_dimension=0, tiled=True)
    grad_response = lax.psum_scatter(
        key_grad[prompt_count:], "ctx", scatter_dimension=0, tiled=True
    )[None]
    token_rows = moe_cot[0]
    block_rows = token_rows.shape[0]
    model_width = token_rows.shape[1]
    top_count = expert_ids.shape[2]
    start = lax.axis_index("ctx") * block_rows
    row_coef = lax.dynamic_slice_in_dim(coefficient, start, block_rows)
    grad_rows = (row_coef[:, None] * token_rows.astype(jnp.float32)).astype(jnp.bfloat16)
    affinity = jax.nn.sigmoid(router_logits[0])
    total = jnp.sum(affinity, axis=1, keepdims=True)
    gate = route_scale * affinity / total
    gate_low = gate.astype(jnp.bfloat16)
    flat_ids = expert_ids[0].reshape(-1)
    entries = flat_ids.shape[0]
    order = jnp.arange(entries, dtype=jnp.int32)
    earlier = (flat_ids[None, :] == flat_ids[:, None]) & (order[None, :] < order[:, None])
    slot_index = jnp.sum(earlier.astype(jnp.int32), axis=1)
    placing = flat_ids * CAP + slot_index
    target = jnp.arange(EXPERTS * CAP, dtype=jnp.int32)
    matches = placing[None, :] == target[:, None]
    filled = jnp.any(matches, axis=1)
    entry_of = jnp.sum(jnp.where(matches, order[None, :], 0), axis=1)
    send_rows = jnp.where(
        filled[:, None],
        jnp.take(grad_rows, entry_of // top_count, axis=0),
        jnp.zeros((), jnp.bfloat16),
    )
    send_gate = jnp.where(
        filled, jnp.take(gate_low.reshape(-1), entry_of), jnp.zeros((), jnp.bfloat16)
    )
    ctx_count = lax.axis_size("ctx")
    resp_count = lax.axis_size("resp")
    devices = ctx_count * resp_count
    per_owner = EXPERTS * CAP // devices
    saved = expert_outputs.reshape(devices, per_owner, model_width)
    arrived, arrived_gate = (
        lax.all_to_all(
            send_rows.reshape(devices, per_owner, model_width),
            ("ctx", "resp"),
            split_axis=0,
            concat_axis=0,
            tiled=True,
        ),
        lax.all_to_all(
            send_gate.reshape(devices, per_owner),
            ("ctx", "resp"),
            split_axis=0,
            concat_axis=0,
            tiled=True,
        ),
    )
    row_grads = (arrived_gate[:, :, None].astype(jnp.float32) * arrived.astype(jnp.float32)).astype(
        jnp.bfloat16
    )
    slot_grad = jnp.einsum("sbd,sbd->sb", arrived, saved, preferred_element_type=jnp.float32)
    returned = lax.all_to_all(slot_grad, ("ctx", "resp"), split_axis=0, concat_axis=0, tiled=True)
    gate_grad = jnp.take(returned.reshape(-1), placing).reshape(block_rows, top_count)
    mixed = jnp.sum(gate_grad * affinity, axis=1, keepdims=True) / total
    grad_router = route_scale / total * (gate_grad - mixed) * affinity * (1.0 - affinity)
    expert_row_grads = row_grads.reshape(expert_outputs.shape)
    return (grad_query, grad_prompt, grad_response, expert_row_grads, grad_router[None])


def solution(mesh):
    placed = (
        P("resp", None, "ctx"),
        P("resp", None, "ctx"),
        P("ctx", None),
        P("resp", None, None),
        P("resp", None),
        P("resp", None),
        P("resp"),
        P("resp", "ctx", None),
        P("resp", "ctx", None),
        P("resp", "ctx", None),
        P(None, ("ctx", "resp"), None, None),
    )
    return jax.shard_map(
        on_device,
        mesh=mesh,
        in_specs=placed,
        out_specs=(
            P("resp", None, "ctx"),
            P(("ctx", "resp"), None),
            P("resp", "ctx", None),
            P(None, ("ctx", "resp"), None, None),
            P("resp", "ctx", None),
        ),
        check_vma=False,
    )
```

profile of v0, /device:TPU:1, one launch (start us, length us, event | category | flops | bytes accessed | tf_op | source)
XLA Modules:
  0.0 424.7 jit_solution(13687672234798176600)
XLA Ops:
  7.2 0.7 all-gather.2.cloned.1.call-update
  7.9 0.8 copy.88
  8.8 0.2 convert_reduce_fusion
  9.0 0.1 select_reduce_fusion
  9.1 0.4 copy-done.16
  9.5 0.2 fusion.21
  9.7 0.1 reduce_sum.83
  9.8 0.1 reduce_or.12
  9.9 0.8 copy.89
  10.7 0.1 fusion.43
  11.1 3.4 gather_fusion
  14.5 0.1 gather.21
  14.7 0.7 copy.90
  15.3 12.0 %all-to-all-start = ((bf16[128,1,4]{2,1,0:T(2,128)(2,1)}), bf16[128,1,4]{2,1,0:T(2,128)(2,1)}, u32[]{:S(2)}, u32[]{:S(2)}) async-start(bf16[128,1,4]{2,1,0:T(2,128)(2,1)} %copy.90), calls=%async_computation | async-start | bytes 131072 | tf_op jit(solution)/shard_map/all_to_all | solution.py:137
  27.3 0.5 broadcast.562
  27.8 1.2 reduce.10
  29.0 0.8 fusion.32
  29.9 0.6 fusion.44
  33.2 0.1 broadcast_in_dim.128
  33.4 4.2 copy.81
  38.3 2.4 copy.80
  41.0 0.1 fusion.20
  41.2 7.1 %gather_fusion.1 = bf16[512,7168]{1,0:T(8,128)(2,1)} fusion(bf16[32,7168]{1,0:T(8,128)(2,1)S(1)} %fusion.20, s32[1024]{0:T(1024)S(1)} %pad_clamp_fusion.1), kind=kCustom, calls=%fused_computation.1 | custom fusion | bytes 14682112 | tf_op jit(solution)/shard_map/jit(_take)/gather | solution.py:118
  48.2 12.6 %gather.23 = bf16[128,4,7168]{2,1,0:T(4,128)(2,1)} reshape(bf16[512,7168]{1,0:T(8,128)(2,1)} %gather_fusion.1) | data formatting | bytes 14680064 | tf_op jit(solution)/shard_map/jit(_take)/gather | solution.py:118
  61.0 0.1 copy.95
  61.1 2.6 fusion.13
  63.7 4.1 multiply_convert_fusion.1
  67.8 10.2 %select_select_fusion = bf16[128,4,7168]{2,1,0:T(4,128)(2,1)} fusion(bf16[128,4,7168]{2,1,0:T(4,128)(2,1)} %gather.23, pred[128,4]{1,0:T(8,128)(4,1)S(1)} %copy.95, pred[128,4]{1,0:T(8,128)(4,1)S(1)} %broadcast_in_dim.128), kind=kLoop, calls=%fused_computation.14 | loop fusion | flops 7340032 | bytes 14681088 | tf_op jit(solution)/shard_map/jit(_where)/select_n | solution.py:116
  78.0 1.6 copy.79
  79.6 9.6 %fusion.18 = f32[1536,512,4]{1,0,2:T(8,128)} fusion(bf16[512,4,576]{0,2,1:T(8,128)(2,1)S(1)} %bitcast.91, bf16[512,576]{0,1:T(8,128)(2,1)} %bitcast.107, bf16[1024,576]{0,1:T(8,128)(2,1)S(1)} %copy.79), kind=kOutput, calls=%fused_computation.36 | convolution fusion | flops 3627417600 | bytes 16711680 | tf_op jit(solution)/shard_map/ihc,jc->hij/dot_general | solution.py:66
  89.2 14.5 %fusion.45 = (f32[4,512]{1,0:T(4,128)}, f32[4,512,1536]{1,2,0:T(8,128)}) fusion(f32[1536,512,4]{1,0,2:T(8,128)} %fusion.18, pred[512,1536]{0,1:T(8,128)(4,1)S(1)} %copy-done.9), kind=kOutput, calls=%fused_computation.110 | output fusion | flops 18875904 | bytes 25960448 | tf_op jit(solution)/shard_map/sub | solution.py:70
  103.8 10.1 %all-to-all-start.1 = ((bf16[128,4,7168]{2,1,0:T(4,128)(2,1)}), bf16[128,4,7168]{2,1,0:T(4,128)(2,1)}, u32[]{:S(2)}, u32[]{:S(2)}) async-start(bf16[128,4,7168]{2,1,0:T(4,128)(2,1)} %select_select_fusion), calls=%async_computation.1 | async-start | bytes 14680064 | tf_op jit(solution)/shard_map/all_to_all | solution.py:130
  114.0 6.4 %fusion.9 = bf16[4,512,1536]{1,2,0:T(8,128)(2,1)S(1)} fusion(f32[4,512,1536]{1,2,0:T(8,128)} %get-tuple-element.41, f32[4,512]{1,0:T(4,128)S(1)} %copy-done.18), kind=kLoop, calls=%fused_computation.19 | loop fusion | flops 6291456 | bytes 18882560 | tf_op jit(solution)/shard_map/convert_element_type | solution.py:72
  120.4 2.7 copy-done
  123.1 5.5 %fusion.10 = f32[512,4]{0,1:T(4,128)S(1)} fusion(bf16[512,4,512]{0,2,1:T(8,128)(2,1)} %multiply_convert_fusion.1, bf16[4,512,1536]{1,2,0:T(8,128)(2,1)S(1)} %fusion.9, bf16[1024,576]{0,1:T(8,128)(2,1)} %copy-done.7, bf16[512,576]{0,1:T(8,128)(2,1)} %bitcast.108), kind=kOutput, calls=%fused_computation.22 | convolution fusion | flops 3227514880 | bytes 10166272 | tf_op jit(solution)/shard_map/hij,jc->ihc/dot_general | solution.py:75
  128.6 8.0 %convolution_bitcast_fusion = f32[1536,512]{0,1:T(8,128)} fusion(bf16[4,512,1536]{1,2,0:T(8,128)(2,1)} %copy-done, bf16[512,4,512]{0,2,1:T(8,128)(2,1)S(1)} %copy-done.5), kind=kOutput, calls=%fused_computation.26 | convolution fusion | flops 3221225472 | bytes 11534336 | tf_op jit(solution)/shard_map/hij,ihc->jc/dot_general | solution.py:86
  136.7 7.7 %fusion.4 = bf16[4,512,1536]{1,2,0:T(8,128)(2,1)} fusion(bf16[512,4,512]{0,2,1:T(8,128)(2,1)S(1)} %copy-done.6, f32[4,512]{1,0:T(4,128)S(1)} %bitcast.111, f32[4,512,1536]{1,2,0:T(8,128)S(1)} %bitcast.90, f32[4,512]{1,0:T(4,128)S(1)} %copy-done.18, bf16[1024,576]{0,1:T(8,128)(2,1)} %copy-done.7, bf16[512,576]{0,1:T(8,128)(2,1)} %bitcast.109), kind=kOutput, calls=%fused_computation.10 | convolution fusion | flops 3236954112 | bytes 22757376 | tf_op jit(solution)/shard_map/ihc,jc->hij/dot_general | solution.py:77
  144.4 7.6 %fusion.11 = f32[1536,576]{0,1:T(8,128)S(1)} fusion(f32[1536,512]{0,1:T(8,128)} %convolution_bitcast_fusion, bf16[4,512,1536]{1,2,0:T(8,128)(2,1)} %fusion.4, bf16[512,4,576]{0,2,1:T(8,128)(2,1)S(1)} %bitcast.92), kind=kOutput, calls=%fused_computation.25 | convolution fusion | flops 3625648128 | bytes 15335424 | tf_op jit(solution)/shard_map/hij,ihc->jc/dot_general | solution.py:83
  152.0 1.8 copy-done.1
  153.9 1.7 slice.30
  155.7 0.7 reduce_sum.87
  156.4 0.7 reduce_sum.89
  157.0 16.8 %reshape.566 = bf16[128,4,7168]{2,1,0:T(4,128)(2,1)} reshape(bf16[128,2,2,7168]{3,2,1,0:T(2,128)(2,1)} %param.21) | data formatting | bytes 14680064 | tf_op jit(solution)/shard_map/reshape | solution.py:128
  174.0 0.6 pad_clamp_fusion
  174.6 1.5 convert_element_type.78
  176.1 1.4 slice.31
  177.5 1.6 copy.115
  179.1 6.8 %multiply_convert_fusion = bf16[576,4,512]{2,0,1:T(8,128)(2,1)S(1)} fusion(bf16[4,512,1536]{1,2,0:T(8,128)(2,1)} %fusion.4, bf16[512,576]{0,1:T(8,128)(2,1)} %bitcast.110, bf16[1024,576]{0,1:T(8,128)(2,1)S(1)} %copy-done.8), kind=kOutput, calls=%fused_computation.20 | convolution fusion | flops 3629776896 | bytes 10420224 | tf_op jit(solution)/shard_map/hij,jc->ihc/dot_general | solution.py:79
  185.9 2.4 copy.97
  188.4 14.0 %all-to-all-done.1 = bf16[128,4,7168]{2,1,0:T(4,128)(2,1)} async-done(((bf16[128,4,7168]{2,1,0:T(4,128)(2,1)}), bf16[128,4,7168]{2,1,0:T(4,128)(2,1)}, u32[]{:S(2)}, u32[]{:S(2)}) %all-to-all-start.1) | async-done | bytes 7340064 | tf_op jit(solution)/shard_map/all_to_all | solution.py:130
  202.3 11.0 %fusion.2 = (f32[128,4]{1,0:T(8,128)}, bf16[128,4,7168]{2,1,0:T(4,128)(2,1)}) fusion(bf16[128,4,7168]{2,1,0:T(4,128)(2,1)} %all-to-all-done.1, bf16[128,4,7168]{2,1,0:T(4,128)(2,1)} %reshape.566, f32[128,4]{1,0:T(8,128)S(1)} %bitcast.95), kind=kLoop, calls=%fused_computation.7 | loop fusion | flops 22019584 | bytes 22024192 | tf_op jit(solution)/shard_map/sbd,sbd->sb/dot_general | solution.py:148
  213.4 12.3 %all-to-all-start.2 = ((f32[128,1,4]{2,1,0:T(1,128)}), f32[128,1,4]{2,1,0:T(1,128)S(1)}, u32[]{:S(2)}, u32[]{:S(2)}) async-start(f32[128,1,4]{2,1,0:T(1,128)} %bitcast.29), calls=%async_computation.2 | async-start | bytes 131072 | tf_op jit(solution)/shard_map/all_to_all | solution.py:149
  225.7 112.0 %all-reduce.4.cloned.1.call-done = f32[1024,576]{0,1:T(8,128)} async-done(((f32[1024,576]{0,1:T(8,128)}), f32[1024,576]{0,1:T(8,128)}) %all-reduce.4.cloned.1.call-update) | async-done | bytes 2359312
  337.7 1.1 constant_dynamic-slice_fusion
  338.8 0.7 copy.98
  339.5 57.3 %reduce-scatter.5.cloned.1.call-done = f32[32,576]{1,0:T(8,128)} async-done(((f32[512,576]{1,0:T(8,128)}), f32[32,576]{1,0:T(8,128)}) %reduce-scatter.5.cloned.1.call-update) | async-done | bytes 73744
  396.8 1.0 copy.116
  397.9 0.8 copy.99
  398.6 15.5 %reshape.565 = bf16[128,2,2,7168]{3,2,1,0:T(2,128)(2,1)} reshape(bf16[128,4,7168]{2,1,0:T(4,128)(2,1)} %get-tuple-element.31) | data formatting | bytes 14680064 | tf_op jit(solution)/shard_map/reshape | solution.py:153
  414.1 0.7 reduce.11
  414.9 0.1 reshape.567
  415.0 2.1 gather_fusion.2
  417.2 0.1 fusion.26
  417.5 0.7 copy.100
  (87 shorter events, 1.5 us)
Async XLA Ops:
  7.2 70.8 %all-gather.2.cloned.1.call-start = ((), (), s32[]{:S(2)}) async-start(), calls=%async_computation.4 | async-start | bytes 1392640 | tf_op jit(solution)/shard_map/all_gather | solution.py:59
  8.9 0.6 copy-start.16
  10.7 22.7 %copy-start.12 = (f32[1,32,8]{2,1,0:T(8,128)}, f32[1,32,8]{2,1,0:T(8,128)S(1)}, u32[]{:S(2)}) copy-start(f32[1,32,8]{2,1,0:T(8,128)S(1)} %copy.89) | copy-start | bytes 3076
  10.8 16.5 %copy-start.19 = (f32[32]{0:T(128)}, f32[32]{0:T(128)S(1)}, u32[]{:S(2)}) copy-start(f32[32]{0:T(128)S(1)} %get-tuple-element.32) | copy-start | bytes 388
  14.5 23.9 %copy-start.2 = (bf16[1,512,2304]{2,1,0:T(8,128)(2,1)S(1)}, bf16[1,512,2304]{2,1,0:T(8,128)(2,1)}, u32[]{:S(2)}) copy-start(bf16[1,512,2304]{2,1,0:T(8,128)(2,1)} %param.11) | copy-start | bytes 7077892
  15.3 88.5 %all-to-all-start = ((bf16[128,1,4]{2,1,0:T(2,128)(2,1)}), bf16[128,1,4]{2,1,0:T(2,128)(2,1)}, u32[]{:S(2)}, u32[]{:S(2)}) async-start(bf16[128,1,4]{2,1,0:T(2,128)(2,1)} %copy.90), calls=%async_computation | async-start | bytes 131072 | tf_op jit(solution)/shard_map/all_to_all | solution.py:137
  37.5 3.4 copy-start.21
  37.5 3.5 copy-start.10
  67.8 11.8 %copy-start.3 = (bf16[1,512,2304]{1,2,0:T(8,128)(2,1)S(1)}, bf16[1,512,2304]{1,2,0:T(8,128)(2,1)}, u32[]{:S(2)}) copy-start(bf16[1,512,2304]{1,2,0:T(8,128)(2,1)} %copy.80) | copy-start | bytes 7077892
  79.6 9.6 %copy-start.7 = (bf16[1024,576]{0,1:T(8,128)(2,1)}, bf16[1024,576]{0,1:T(8,128)(2,1)S(1)}, u32[]{:S(2)}) copy-start(bf16[1024,576]{0,1:T(8,128)(2,1)S(1)} %copy.79) | copy-start | bytes 3538948
  79.6 9.6 %copy-start.9 = (pred[512,1536]{0,1:T(8,128)(4,1)S(1)}, pred[512,1536]{0,1:T(8,128)(4,1)}, u32[]{:S(2)}) copy-start(pred[512,1536]{0,1:T(8,128)(4,1)} %fusion.13) | copy-start | bytes 2359300
  103.8 10.2 %copy-start.18 = (f32[4,512]{1,0:T(4,128)S(1)}, f32[4,512]{1,0:T(4,128)}, u32[]{:S(2)}) copy-start(f32[4,512]{1,0:T(4,128)} %get-tuple-element.40) | copy-start | bytes 24580
  103.8 98.5 %all-to-all-start.1 = ((bf16[128,4,7168]{2,1,0:T(4,128)(2,1)}), bf16[128,4,7168]{2,1,0:T(4,128)(2,1)}, u32[]{:S(2)}, u32[]{:S(2)}) async-start(bf16[128,4,7168]{2,1,0:T(4,128)(2,1)} %select_select_fusion), calls=%async_computation.1 | async-start | bytes 14680064 | tf_op jit(solution)/shard_map/all_to_all | solution.py:130
  113.9 223.7 %all-reduce.4.cloned.1.call-start = ((), (), s32[]{:S(2)}) async-start(), calls=%async_computation.6 | async-start | bytes 4718592
  120.4 2.7 copy-start
  123.1 5.5 %copy-start.5 = (bf16[512,4,512]{0,2,1:T(8,128)(2,1)S(1)}, bf16[512,4,512]{0,2,1:T(8,128)(2,1)}, u32[]{:S(2)}) copy-start(bf16[512,4,512]{0,2,1:T(8,128)(2,1)} %multiply_convert_fusion.1) | copy-start | bytes 6291460
  123.1 13.6 %slice-start = ((s8[12582912]{0:T(1024)(128)(4,1)}), s8[4194304]{0:T(1024)(128)(4,1)S(1)}, s32[]{:S(2)}) async-start(s8[12582912]{0:T(1024)(128)(4,1)} %bitcast.89), calls=%async_computation.7 | async-start | bytes 8388608
  123.1 13.6 %slice-start.1 = ((s8[12582912]{0:T(1024)(128)(4,1)}), s8[4194304]{0:T(1024)(128)(4,1)S(1)}, s32[]{:S(2)}) async-start(s8[12582912]{0:T(1024)(128)(4,1)} %bitcast.89), calls=%async_computation.8 | async-start | bytes 8388608
  128.6 8.1 %slice-start.2 = ((s8[12582912]{0:T(1024)(128)(4,1)}), s8[4194304]{0:T(1024)(128)(4,1)S(1)}, s32[]{:S(2)}) async-start(s8[12582912]{0:T(1024)(128)(4,1)} %bitcast.89), calls=%async_computation.9 | async-start | bytes 8388608
  128.6 8.1 %copy-start.6 = (bf16[512,4,512]{0,2,1:T(8,128)(2,1)S(1)}, bf16[512,4,512]{0,2,1:T(8,128)(2,1)}, u32[]{:S(2)}) copy-start(bf16[512,4,512]{0,2,1:T(8,128)(2,1)} %multiply_convert_fusion.1) | copy-start | bytes 6291460
  136.7 7.7 %copy-start.4 = (bf16[1,512,2304]{1,2,0:T(8,128)(2,1)S(1)}, bf16[1,512,2304]{1,2,0:T(8,128)(2,1)}, u32[]{:S(2)}) copy-start(bf16[1,512,2304]{1,2,0:T(8,128)(2,1)} %copy.80) | copy-start | bytes 7077892
  152.0 1.9 copy-start.1
  153.9 1.8 copy-start.17
  155.6 241.2 %reduce-scatter.5.cloned.1.call-start = ((), (), s32[]{:S(2)}) async-start(), calls=%async_computation.5 | async-start | bytes 1392640
  173.9 5.2 %copy-start.8 = (bf16[1024,576]{0,1:T(8,128)(2,1)S(1)}, bf16[1024,576]{0,1:T(8,128)(2,1)}, u32[]{:S(2)}) copy-start(bf16[1024,576]{0,1:T(8,128)(2,1)} %copy-done.7) | copy-start | bytes 3538948
  185.9 16.4 %copy-start.11 = (f32[128,1,4]{2,1,0:T(1,128)S(1)}, f32[128,1,4]{2,1,0:T(1,128)}, u32[]{:S(2)}) copy-start(f32[128,1,4]{2,1,0:T(1,128)} %convert_element_type.78) | copy-start | bytes 6148
  213.4 200.8 %all-to-all-start.2 = ((f32[128,1,4]{2,1,0:T(1,128)}), f32[128,1,4]{2,1,0:T(1,128)S(1)}, u32[]{:S(2)}, u32[]{:S(2)}) async-start(f32[128,1,4]{2,1,0:T(1,128)} %bitcast.29), calls=%async_computation.2 | async-start | bytes 131072 | tf_op jit(solution)/shard_map/all_to_all | solution.py:149
  398.6 18.6 %copy-start.13 = (f32[1,32,8]{2,1,0:T(8,128)S(1)}, f32[1,32,8]{2,1,0:T(8,128)}, u32[]{:S(2)}) copy-start(f32[1,32,8]{2,1,0:T(8,128)} %copy-done.12) | copy-start | bytes 3076
  398.6 18.6 %copy-start.15 = (s32[32,8]{1,0:T(8,128)S(1)}, s32[32,8]{1,0:T(8,128)}, u32[]{:S(2)}) copy-start(s32[32,8]{1,0:T(8,128)} %reduce_sum.89) | copy-start | bytes 3076
  398.6 18.7 %copy-start.20 = (f32[32]{0:T(128)S(1)}, f32[32]{0:T(128)}, u32[]{:S(2)}) copy-start(f32[32]{0:T(128)} %copy-done.19) | copy-start | bytes 388
  398.6 18.8 %copy-start.14 = (s32[1,32,8]{2,1,0:T(8,128)S(1)}, s32[1,32,8]{2,1,0:T(8,128)}, u32[]{:S(2)}) copy-start(s32[1,32,8]{2,1,0:T(8,128)} %reduce_sum.87) | copy-start | bytes 3076
Sparse Core Ops, SparseCore 0:
  9.7 36.5 all-gather.1
  155.7 181.9 all-reduce.3
  340.2 56.5 reduce-scatter.4
where the time goes:
time: 430 us; the launch traced here: 425 us
  waiting for transfers between devices  184 us (43%)
  local copies, waits for them, and re-layouts  88.4 us (21%)
  other arithmetic  54.9 us (13%)
  matrix products  45.3 us (11%)
  starting transfers between devices  34.5 us (8%)
  between operations  17.6 us (4%)
    unnamed x5, waiting for transfers between devices  170 us
    gather x2, local copies, waits for them, and re-layouts, on_device(): jnp.take(grad_rows, entry_of // top_count, axis=0)  19.7 us
    unnamed x63, local copies, waits for them, and re-layouts  17.8 us
    reshape x1, local copies, waits for them, and re-layouts, on_device(): saved = expert_outputs.reshape(devices, per_owner, model_width)  16.8 us
    reshape x1, local copies, waits for them, and re-layouts, on_device(): expert_row_grads = row_grads.reshape(expert_outputs.shape)  15.5 us
    sub x1, other arithmetic, on_device(): exponent = jnp.exp(scores - row_top)  14.5 us
    all_to_all x1, waiting for transfers between devices, on_device(): lax.all_to_all(send_rows.reshape(devices, per_owner, model_width), ('ctx'...  14 us
    all_to_all x1, starting transfers between devices, on_device(): lax.all_to_all(slot_grad, ('ctx', 'resp'), split_axis=0, concat_axis=0, t...  12.3 us
  transfers between devices with their start and end apart: 6, of which 3 were waited for; matrix products, arithmetic and copies ran while one was open for 42% of the time, Pallas kernels for 0%

commit v1 on v0

v1 whole, which is shorter than its diff:
```python
import jax
import jax.numpy as jnp
from jax import lax
from jax.experimental import pallas as pl
from jax.experimental.pallas import tpu as pltpu
from jax.sharding import PartitionSpec as P

EXPERTS = 256
CAP = 2
LANES = 128

score_scale = 192.0 ** (-0.5)
preference_beta = 0.5
route_scale = 2.5
log2_e = 1.4426950408889634

f32 = jnp.float32
bf16 = jnp.bfloat16


def coefficient_row(ratio_ref, lengths_ref, chosen_ref):
    rows = ratio_ref.shape[1]
    half = rows // 2
    lane = lax.broadcasted_iota(jnp.int32, (1, rows), 1)
    second = lane >= half
    position = jnp.where(second, lane - half, lane)
    length = jnp.where(second, lengths_ref[0, 1], lengths_ref[0, 0])
    live = position < length
    ratios = jnp.where(live, ratio_ref[...], 0.0)
    first_total = jnp.sum(jnp.where(second, 0.0, ratios), axis=1, keepdims=True)
    second_total = jnp.sum(jnp.where(second, ratios, 0.0), axis=1, keepdims=True)
    chosen = chosen_ref[0]
    margin = first_total - second_total
    margin = jnp.where(chosen == 0, margin, -margin)
    weight = preference_beta * jax.nn.sigmoid(-preference_beta * margin)
    signed = jnp.where(second == (chosen == 1), -weight, weight)
    return jnp.where(live, signed, 0.0)


def column_of(row):
    n = row.shape[1]
    return jnp.transpose(jnp.broadcast_to(row, (8, n)))[:, :1]


def router_gates(logits):
    affinity = jax.nn.sigmoid(logits)
    total = jnp.sum(affinity, axis=0, keepdims=True)
    return affinity, total, route_scale * affinity / total


def send_kernel(
    lengths_ref, chosen_ref, start_ref, ratio_ref, ids_ref, logits_ref, cot_ref,
    send_ref, slot_ref, rows_ref, pair_ref, table_ref, gates_ref, table_smem, gates_smem, sems,
):
    tokens, model = cot_ref.shape
    top = ids_ref.shape[0]
    tiles = model // LANES
    per_step = EXPERTS // pl.num_programs(0)

    @pl.when(pl.program_id(0) == 0)
    def _():
        _, _, gate = router_gates(logits_ref[...])
        gate = gate.astype(bf16).astype(f32)
        ids = jnp.transpose(ids_ref[...])
        gates = jnp.transpose(gate)
        expert = lax.broadcasted_iota(jnp.int32, (tokens, EXPERTS), 1)
        named = jnp.zeros((tokens, EXPERTS), f32)
        weight = jnp.zeros((tokens, EXPERTS), f32)
        for n in range(top):
            hit = ids[:, n : n + 1] == expert
            named = jnp.where(hit, 1.0, named)
            weight = jnp.where(hit, gates[:, n : n + 1], weight)
        row_i = lax.broadcasted_iota(jnp.int32, (tokens, tokens), 0)
        col_i = lax.broadcasted_iota(jnp.int32, (tokens, tokens), 1)
        before = jnp.dot(
            (col_i < row_i).astype(bf16), named.astype(bf16), preferred_element_type=f32
        )
        token = lax.broadcasted_iota(jnp.int32, (tokens, EXPERTS), 0).astype(f32)
        for s in range(CAP):
            here = jnp.where((before == float(s)) & (named > 0.0), 1.0, 0.0)
            table_ref[s : s + 1, :] = jnp.sum(here * token, axis=0, keepdims=True).astype(jnp.int32)
            gates_ref[s : s + 1, :] = jnp.sum(here * weight, axis=0, keepdims=True)
        table_copy = pltpu.make_async_copy(table_ref, table_smem, sems.at[0])
        gates_copy = pltpu.make_async_copy(gates_ref, gates_smem, sems.at[1])
        table_copy.start()
        gates_copy.start()
        slots = []
        for n in range(top):
            hit = ids[:, n : n + 1] == expert
            slots.append(jnp.sum(jnp.where(hit, before, 0.0), axis=1, keepdims=True))
        slot_ref[...] = jnp.transpose(jnp.concatenate(slots, axis=1)).astype(jnp.int32)
        coefficient = coefficient_row(ratio_ref, lengths_ref, chosen_ref)
        lane = lax.broadcasted_iota(jnp.int32, (tokens, coefficient.shape[1]), 1)
        row = lax.broadcasted_iota(jnp.int32, (tokens, coefficient.shape[1]), 0)
        own = jnp.sum(
            jnp.where(lane == row + start_ref[0], coefficient, 0.0), axis=1, keepdims=True
        )
        for tile in range(tiles):
            cot = cot_ref[:, tile * LANES : (tile + 1) * LANES].astype(f32)
            rows_ref[pl.ds(tile, tokens, stride=tiles), :] = (own * cot).astype(bf16).astype(f32)
        table_copy.wait()
        gates_copy.wait()

    first = pl.program_id(0) * per_step

    def place(e, carry):
        for s in range(CAP):
            token = table_smem[s, first + e]
            block = rows_ref[pl.ds(pl.multiple_of(token * tiles, 8), tiles), :]
            pair_ref[pl.ds(s, tiles, stride=CAP), :] = block * gates_smem[s, first + e]
        at = pl.multiple_of(e * (tiles * CAP), 16)
        send_ref[pl.ds(at, tiles * CAP), :] = pair_ref[...].astype(bf16)
        return carry

    lax.fori_loop(0, per_step, place, 0, unroll=4)


def build_send(lengths, chosen, start, ratio, ids, logits, cot):
    tokens, model = cot.shape
    tiles = model // LANES
    rows = EXPERTS * CAP * tiles
    steps = 8
    whole = lambda shape: pl.BlockSpec(shape, lambda i: (0, 0))
    smem = pl.BlockSpec(memory_space=pltpu.SMEM)
    return pl.pallas_call(
        send_kernel,
        grid=(steps,),
        in_specs=[
            smem, smem, smem,
            whole(ratio.shape), whole(ids.shape), whole(logits.shape), whole(cot.shape),
        ],
        out_specs=[
            pl.BlockSpec((rows // steps, LANES), lambda i: (i, 0)),
            whole(ids.shape),
        ],
        out_shape=[
            jax.ShapeDtypeStruct((rows, LANES), bf16),
            jax.ShapeDtypeStruct(ids.shape, jnp.int32),
        ],
        scratch_shapes=[
            pltpu.VMEM((tokens * tiles, LANES), f32),
            pltpu.VMEM((tiles * CAP, LANES), f32),
            pltpu.VMEM((8, EXPERTS), jnp.int32),
            pltpu.VMEM((8, EXPERTS), f32),
            pltpu.SMEM((8, EXPERTS), jnp.int32),
            pltpu.SMEM((8, EXPERTS), f32),
            pltpu.SemaphoreType.DMA((2,)),
        ],
        compiler_params=pltpu.CompilerParams(vmem_limit_bytes=32 << 20),
        cost_estimate=pl.CostEstimate(flops=0, bytes_accessed=8_000_000, transcendentals=0),
        name="build_send",
    )(lengths, chosen, start, ratio, ids, logits, cot)


def dot_kernel(got_ref, saved_ref, out_ref):
    rows = got_ref.shape[0]
    pairs = out_ref.shape[0]
    tall = rows // pairs
    product = got_ref[...].astype(f32) * saved_ref[...].astype(f32)
    product = jnp.sum(product.reshape(pairs, tall // 8, 8, LANES), axis=1)
    out_ref[...] = jnp.sum(product, axis=2)


def slot_dots(got, saved, tiles):
    pairs = got.shape[0] // (tiles * CAP)
    steps = 8
    spec = pl.BlockSpec((got.shape[0] // steps, LANES), lambda i: (i, 0))
    return pl.pallas_call(
        dot_kernel,
        grid=(steps,),
        in_specs=[spec, spec],
        out_specs=pl.BlockSpec((pairs // steps, 8), lambda i: (i, 0)),
        out_shape=jax.ShapeDtypeStruct((pairs, 8), f32),
        compiler_params=pltpu.CompilerParams(vmem_limit_bytes=32 << 20),
        cost_estimate=pl.CostEstimate(flops=8_000_000, bytes_accessed=15_000_000, transcendentals=0),
        name="slot_dots",
    )(got, saved)


NT = (((1,), (1,)), ((), ()))


def attention_kernel(
    lengths_ref, chosen_ref, ratio_ref, q_ref, cot_ref, prompt_ref, answer_ref,
    gq_ref, send_ref, keys_ref, keys_t_ref, acc_ref, value_ref,
):
    prompt_count, width = prompt_ref.shape
    row_count = answer_ref.shape[1]
    half = row_count // 2
    wide = keys_ref.shape[2]
    rank = value_ref.shape[1]
    pad = wide - width
    step = pl.program_id(0)

    @pl.when(step == 0)
    def _():
        answer_t = answer_ref[...]
        keys_t_ref[:, :prompt_count] = jnp.transpose(prompt_ref[...])
        keys_t_ref[:, prompt_count:] = answer_t
        latent = jnp.concatenate([prompt_ref[...], jnp.transpose(answer_t)], axis=0)
        zeros = jnp.zeros((latent.shape[0], pad), bf16)
        keys_ref[0] = jnp.concatenate([latent, zeros], axis=1)
        keys_ref[1] = jnp.concatenate([zeros, latent], axis=1)
        acc_ref[...] = jnp.zeros_like(acc_ref)
        value_ref[...] = jnp.zeros_like(value_ref)

    coefficient = column_of(coefficient_row(ratio_ref, lengths_ref, chosen_ref))
    key_i = lax.broadcasted_iota(jnp.int32, (half, half), 0)
    row_i = lax.broadcasted_iota(jnp.int32, (half, half), 1)
    causal = key_i <= row_i
    for k in range(2):
        rows = slice(k * half, (k + 1) * half)
        answer = slice(prompt_count + k * half, prompt_count + (k + 1) * half)
        grads = []
        for h in range(2):
            query = q_ref[rows, h * rank : h * rank + wide]
            grad_out = (
                coefficient[rows] * cot_ref[rows, h * rank : (h + 1) * rank].astype(f32)
            ).astype(bf16)
            s_prompt = lax.dot_general(
                keys_ref[h, :prompt_count], query, NT, preferred_element_type=f32
            )
            s_answer = lax.dot_general(keys_ref[h, answer], query, NT, preferred_element_type=f32)
            s_answer = jnp.where(causal, s_answer, -1e30)
            top = jnp.maximum(
                jnp.max(s_prompt, axis=0, keepdims=True), jnp.max(s_answer, axis=0, keepdims=True)
            )
            e_prompt = jnp.exp2((s_prompt - top) * (score_scale * log2_e))
            e_answer = jnp.exp2((s_answer - top) * (score_scale * log2_e))
            total = jnp.sum(e_prompt, axis=0, keepdims=True) + jnp.sum(
                e_answer, axis=0, keepdims=True
            )
            inverse = 1.0 / total
            p_prompt = e_prompt * inverse
            p_answer = e_answer * inverse
            b_prompt = p_prompt.astype(bf16)
            b_answer = p_answer.astype(bf16)
            d_prompt = lax.dot_general(
                keys_ref[0, :prompt_count, :rank], grad_out, NT, preferred_element_type=f32
            )
            d_answer = lax.dot_general(
                keys_ref[0, answer, :rank], grad_out, NT, preferred_element_type=f32
            )
            delta = jnp.sum(b_prompt.astype(f32) * d_prompt, axis=0, keepdims=True) + jnp.sum(
                b_answer.astype(f32) * d_answer, axis=0, keepdims=True
            )
            g_prompt = (p_prompt * (d_prompt - delta)).astype(bf16)
            g_answer = (p_answer * (d_answer - delta)).astype(bf16)
            grads.append(
                jnp.dot(keys_t_ref[:, :prompt_count], g_prompt, preferred_element_type=f32)
                + jnp.dot(keys_t_ref[:, answer], g_answer, preferred_element_type=f32)
            )
            acc_ref[h, :prompt_count] += jnp.dot(g_prompt, query, preferred_element_type=f32)
            acc_ref[h, answer] += jnp.dot(g_answer, query, preferred_element_type=f32)
            value_ref[:prompt_count] += jnp.dot(b_prompt, grad_out, preferred_element_type=f32)
            value_ref[answer] += jnp.dot(b_answer, grad_out, preferred_element_type=f32)
        both = (score_scale * jnp.concatenate(grads, axis=0)).astype(bf16)
        gq_ref[rows, :] = jnp.transpose(both)

    @pl.when(step == pl.num_programs(0) - 1)
    def _():
        chunks, _, _ = send_ref.shape
        prompt_rows = prompt_count // chunks
        answer_rows = row_count // chunks

        def combined(start, size):
            at = pl.ds(start, size)
            key = acc_ref[0, at, :width] + pltpu.roll(acc_ref[1, at, :], wide - pad, 1)[:, :width]
            value = jnp.concatenate([value_ref[at, :], jnp.zeros((size, width - rank), f32)], axis=1)
            return (score_scale * key + value).astype(bf16)

        for c in range(chunks):
            send_ref[c, :prompt_rows] = combined(c * prompt_rows, prompt_rows)
            send_ref[c, prompt_rows:] = combined(prompt_count + c * answer_rows, answer_rows)


def attention(lengths, chosen, ratio, queries, cot, prompt, answer_t, chunks):
    rows, q_width = queries.shape
    prompt_count, width = prompt.shape
    heads = q_width // width
    rank = cot.shape[1] // heads
    wide = width + width - rank
    steps = heads // 2
    keys = prompt_count + rows
    whole = lambda shape: pl.BlockSpec(shape, lambda i: (0,) * len(shape))
    smem = pl.BlockSpec(memory_space=pltpu.SMEM)
    return pl.pallas_call(
        attention_kernel,
        grid=(steps,),
        in_specs=[
            smem, smem, whole(ratio.shape),
            pl.BlockSpec((rows, 2 * width), lambda i: (0, i)),
            pl.BlockSpec((rows, 2 * rank), lambda i: (0, i)),
            whole(prompt.shape), whole(answer_t.shape),
        ],
        out_specs=[
            pl.BlockSpec((rows, 2 * width), lambda i: (0, i)),
            whole((chunks, keys // chunks, width)),
        ],
        out_shape=[
            jax.ShapeDtypeStruct(queries.shape, bf16),
            jax.ShapeDtypeStruct((chunks, keys // chunks, width), bf16),
        ],
        scratch_shapes=[
            pltpu.VMEM((2, keys, wide), bf16),
            pltpu.VMEM((width, keys), bf16),
            pltpu.VMEM((2, keys, wide), f32),
            pltpu.VMEM((keys, rank), f32),
        ],
        compiler_params=pltpu.CompilerParams(vmem_limit_bytes=50 << 20),
        cost_estimate=pl.CostEstimate(
            flops=17_000_000_000, bytes_accessed=9_000_000, transcendentals=2_600_000
        ),
        name="attention",
    )(lengths, chosen, ratio, queries, cot, prompt, answer_t)


def flat(x):
    n, e, s, d = x.shape
    t = d // LANES
    return x.reshape(n, e, s, t, LANES).transpose(0, 1, 3, 2, 4).reshape(n * e * t * s, LANES)


def unflat(x, n, e, s, d):
    t = d // LANES
    return x.reshape(n, e, t, s, LANES).transpose(0, 1, 3, 2, 4).reshape(n, e, s, d)


def on_device(
    queries,
    attn_cot,
    prompt_latent,
    response_latent,
    log_ratio,
    lengths,
    chosen,
    moe_cot,
    expert_ids,
    router_logits,
    expert_outputs,
):
    ctx_count = lax.axis_size("ctx")
    resp_count = lax.axis_size("resp")
    devices = ctx_count * resp_count
    width = prompt_latent.shape[1]
    tokens, model = moe_cot.shape[1:]
    per_owner = EXPERTS // devices
    start = (lax.axis_index("ctx") * tokens).astype(jnp.int32).reshape(1)
    ids = expert_ids[0].T
    logits = router_logits[0].T

    copies = jnp.broadcast_to(prompt_latent[None], (ctx_count,) + prompt_latent.shape)
    prompt = lax.all_to_all(copies, "ctx", 0, 0, tiled=True).reshape(-1, width)

    sent, slot = build_send(lengths, chosen, start, log_ratio, ids, logits, moe_cot[0])
    arrived = lax.all_to_all(
        unflat(sent, devices, per_owner, CAP, model), ("ctx", "resp"), 0, 0, tiled=True
    )

    grad_query, key_send = attention(
        lengths, chosen, log_ratio, queries[0], attn_cot[0], prompt, response_latent[0].T, ctx_count
    )
    key_rows = lax.all_to_all(key_send, "ctx", 0, 0, tiled=True).astype(f32).sum(axis=0)
    prompt_rows = prompt_latent.shape[0]
    grad_response = key_rows[prompt_rows:][None]
    prompt_part = key_rows[:prompt_rows].reshape(resp_count, prompt_rows // resp_count, width)
    grad_prompt = lax.all_to_all(prompt_part, "resp", 0, 0, tiled=True).sum(axis=0)

    dots = slot_dots(flat(arrived), flat(expert_outputs), model // LANES)
    dots = dots.reshape(devices, per_owner, 4, CAP).sum(axis=2)
    returned = lax.all_to_all(dots, ("ctx", "resp"), 0, 0, tiled=True)

    affinity, total, gate = router_gates(logits)
    gate_low = gate.astype(bf16).astype(f32)
    placing = (ids * CAP + slot).reshape(-1)
    gate_grad = jnp.take(returned.reshape(-1), placing).reshape(ids.shape) / gate_low
    mixed = jnp.sum(gate_grad * affinity, axis=0, keepdims=True) / total
    grad_router = route_scale / total * (gate_grad - mixed) * affinity * (1.0 - affinity)
    return (grad_query[None], grad_prompt, grad_response, arrived, grad_router.T[None])


def solution(mesh):
    placed = (
        P("resp", None, "ctx"),
        P("resp", None, "ctx"),
        P("ctx", None),
        P("resp", None, None),
        P("resp", None),
        P("resp", None),
        P("resp"),
        P("resp", "ctx", None),
        P("resp", "ctx", None),
        P("resp", "ctx", None),
        P(None, ("ctx", "resp"), None, None),
    )
    return jax.shard_map(
        on_device,
        mesh=mesh,
        in_specs=placed,
        out_specs=(
            P("resp", None, "ctx"),
            P(("ctx", "resp"), None),
            P("resp", "ctx", None),
            P(None, ("ctx", "resp"), None, None),
            P("resp", "ctx", None),
        ),
        check_vma=False,
    )
```

time: 430 us -> 234 us (0.54); the launches traced: 425 us -> 234 us
  local copies, waits for them, and re-layouts: 88.4 us -> 21.4 us
  other arithmetic: 54.9 us -> 1.68 us
  waiting for transfers between devices: 184 us -> 131 us
  matrix products: 45.3 us -> 0 us
  Pallas kernels: 0 us -> 40.8 us
  between operations: 17.6 us -> 1.44 us
    unnamed x5 -> x0, waiting for transfers between devices: 170 us -> none
    all_to_all x3 -> x5, waiting for transfers between devices: 14 us -> 131 us  [the longest x1 86.4 us: on_device(): lax.all_to_all(unflat(sent, devices, per_owner, CAP, model), ('ctx', 'res...]
    dot_general x6 -> x0, matrix products: 45.3 us -> none  [the longest x1 9.61 us: on_device(): jnp.einsum('ihc,jc->hij', query, key_rows, preferred_element_type=jnp.flo...]
    pallas_call x0 -> x3, Pallas kernels: none -> 40.8 us  [the longest x1 29.5 us: attention(): pl.pallas_call(attention_kernel, grid=(steps,), in_specs=[smem, smem, who...]
    reshape x3, local copies, waits for them, and re-layouts: 32.3 us -> 1.23 us  [the longest x1 0.67 us: on_device(): key_rows[:prompt_rows].reshape(resp_count, prompt_rows // resp_count, width)]
    gather x7 -> x2, local copies, waits for them, and re-layouts: 25.4 us -> 2.02 us  [on_device(): jnp.take(returned.reshape(-1), placing).reshape(ids.shape) / gate_low]
    sub x1 -> x0, other arithmetic: 14.5 us -> none  [on_device(): exponent = jnp.exp(scores - row_top)]
    convert_element_type x5 -> x0, other arithmetic: 12.2 us -> none  [the longest x1 6.41 us: on_device(): soft_rounded = soft_weights.astype(jnp.bfloat16)]
  transfers between devices with their start and end apart: 6 -> 5, of which waited for: 3 -> 4; matrix products, arithmetic and copies ran while one was open for 42% -> 2% of each run, Pallas kernels for 0% -> 5%
where the time goes in v1:
time: 234 us
  waiting for transfers between devices  131 us (56%)
  Pallas kernels  40.8 us (17%)
  starting transfers between devices  37.5 us (16%)
  local copies, waits for them, and re-layouts  21.4 us (9%)
    all_to_all x1, waiting for transfers between devices, on_device(): lax.all_to_all(unflat(sent, devices, per_owner, CAP, model), ('ctx', 'res...  86.4 us
    pallas_call x1, Pallas kernels, attention(): pl.pallas_call(attention_kernel, grid=(steps,), in_specs=[smem, smem, who...  29.5 us
    all_to_all x1, waiting for transfers between devices, on_device(): prompt = lax.all_to_all(copies, 'ctx', 0, 0, tiled=True).reshape(-1, width)  18 us
    all_to_all x1, waiting for transfers between devices, on_device(): lax.all_to_all(key_send, 'ctx', 0, 0, tiled=True).astype(f32).sum(axis=0)  18 us
    unnamed x17, local copies, waits for them, and re-layouts  13.4 us
    all_to_all x1, starting transfers between devices, on_device(): lax.all_to_all(unflat(sent, devices, per_owner, CAP, model), ('ctx', 'res...  9.8 us
    all_to_all x1, starting transfers between devices, on_device(): returned = lax.all_to_all(dots, ('ctx', 'resp'), 0, 0, tiled=True)  9.44 us
    all_to_all x1, waiting for transfers between devices, on_device(): returned = lax.all_to_all(dots, ('ctx', 'resp'), 0, 0, tiled=True)  8.63 us
  transfers between devices with their start and end apart: 5, of which 4 were waited for; matrix products, arithmetic and copies ran while one was open for 2% of the time, Pallas kernels for 5%

profile of v1, /device:TPU:1, one launch (start us, length us, event | category | flops | bytes accessed | tf_op | source)
XLA Modules:
  0.0 233.8 jit_solution(6136139315627582884)
XLA Ops:
  0.6 0.0 copy-start.5
  0.6 0.0 copy-start.6
  0.7 0.0 copy-start.7
  0.7 2.2 broadcast_in_dim.23
  2.8 7.3 %all-to-all-start = ((bf16[16,64,576]{2,1,0:T(8,128)(2,1)}), bf16[16,64,576]{2,1,0:T(8,128)(2,1)S(1)}, u32[]{:S(2)}, u32[]{:S(2)}) async-start(bf16[16,64,576]{2,1,0:T(8,128)(2,1)} %broadcast_in_dim.23), calls=%async_computation | async-start | bytes 2621440 | tf_op jit(solution)/shard_map/all_to_all | solution.py:353
  10.8 18.0 %all-to-all-done = bf16[16,64,576]{2,1,0:T(8,128)(2,1)S(1)} async-done(((bf16[16,64,576]{2,1,0:T(8,128)(2,1)}), bf16[16,64,576]{2,1,0:T(8,128)(2,1)S(1)}, u32[]{:S(2)}, u32[]{:S(2)}) %all-to-all-start) | async-done | bytes 1179680 | tf_op jit(solution)/shard_map/all_to_all | solution.py:353
  28.8 0.0 copy-done.5
  28.8 0.0 copy-done.6
  28.8 0.0 copy-done.7
  28.8 29.5 %attention.1 = (bf16[512,2304]{1,0:T(8,128)(2,1)}, bf16[16,96,576]{2,1,0:T(8,128)(2,1)}) custom-call(s32[1,2]{1,0:T(1,128)S(1)} %copy-done.6, s32[1]{0:T(128)S(6)} %copy.35.chosen_ref, f32[1,512]{1,0:T(1,128)S(1)} %copy-done.5, bf16[512,2304]{1,0:T(8,128)(2,1)} %bitcast.57, bf16[512,2048]{1,0:T(8,128)(2,1)} %bitcast.58, bf16[1024,576]{1,0:T(8,128)(2,1)S(1)} %bitcast.51, ...), custom_call_target="tpu_custom_call" | custom-call | flops 16999999488 | bytes 9000000 | tf_op jit(solution)/shard_map/attention/pallas_call | solution.py:287
  58.3 0.0 copy-start.2
  58.3 0.0 copy-start.3
  58.3 0.0 copy-start.4
  58.3 4.4 %all-to-all-start.1 = ((bf16[16,96,576]{2,1,0:T(8,128)(2,1)}), bf16[16,96,576]{2,1,0:T(8,128)(2,1)S(1)}, u32[]{:S(2)}, u32[]{:S(2)}) async-start(bf16[16,96,576]{2,1,0:T(8,128)(2,1)} %get-tuple-element.10), calls=%async_computation.1 | async-start | bytes 3932160 | tf_op jit(solution)/shard_map/all_to_all | solution.py:363
  62.7 0.0 copy-done.2
  62.7 0.0 copy-done.3
  62.7 0.0 copy-done.4
  62.7 4.9 %build_send.1 = (bf16[28672,128]{1,0:T(8,128)(2,1)S(1)}, s32[8,32]{1,0:T(8,128)S(1)}) custom-call(s32[1,2]{1,0:T(1,128)S(1)} %copy-done.6, s32[1]{0:T(128)S(6)} %copy.35.chosen_ref, s32[1]{0:T(128)} %bitcast.8.start_ref, f32[1,512]{1,0:T(1,128)S(1)} %copy-done.5, s32[8,32]{1,0:T(8,128)S(1)} %bitcast.54, f32[8,32]{1,0:T(8,128)S(1)} %bitcast.53, ...), custom_call_target="tpu_custom_call" | custom-call | bytes 8000000 | tf_op jit(solution)/shard_map/build_send/pallas_call | solution.py:125
  67.6 0.0 copy-start.1
  67.6 3.0 %copy-done.1 = bf16[28672,128]{1,0:T(8,128)(2,1)} copy-done((bf16[28672,128]{1,0:T(8,128)(2,1)}, bf16[28672,128]{1,0:T(8,128)(2,1)S(1)}, u32[]{:S(2)}) %copy-start.1) | copy-done | bytes 7340056
  70.6 18.0 %all-to-all-done.1 = bf16[16,96,576]{2,1,0:T(8,128)(2,1)S(1)} async-done(((bf16[16,96,576]{2,1,0:T(8,128)(2,1)}), bf16[16,96,576]{2,1,0:T(8,128)(2,1)S(1)}, u32[]{:S(2)}, u32[]{:S(2)}) %all-to-all-start.1) | async-done | bytes 1769504 | tf_op jit(solution)/shard_map/all_to_all | solution.py:363
  88.6 9.8 %all-to-all-start.3 = ((bf16[128,2,2,7168]{3,2,1,0:T(2,128)(2,1)}), bf16[128,2,2,7168]{3,2,1,0:T(2,128)(2,1)}, u32[]{:S(2)}, u32[]{:S(2)}) async-start(bf16[128,2,2,7168]{3,2,1,0:T(2,128)(2,1)} %bitcast.50), calls=%async_computation.3 | async-start | bytes 14680064 | tf_op jit(solution)/shard_map/all_to_all | solution.py:356
  98.4 0.1 reshape.105
  98.5 0.3 convert_reduce_fusion
  98.8 0.7 slice_bitcast_fusion
  99.5 86.4 %all-to-all-done.3 = bf16[128,2,2,7168]{3,2,1,0:T(2,128)(2,1)} async-done(((bf16[128,2,2,7168]{3,2,1,0:T(2,128)(2,1)}), bf16[128,2,2,7168]{3,2,1,0:T(2,128)(2,1)}, u32[]{:S(2)}, u32[]{:S(2)}) %all-to-all-start.3) | async-done | bytes 7340064 | tf_op jit(solution)/shard_map/all_to_all | solution.py:356
  185.8 6.5 %all-to-all-start.2 = ((f32[8,8,576]{2,1,0:T(8,128)}), f32[8,8,576]{2,1,0:T(8,128)S(1)}, u32[]{:S(2)}, u32[]{:S(2)}) async-start(f32[8,8,576]{2,1,0:T(8,128)} %slice_bitcast_fusion), calls=%async_computation.2 | async-start | bytes 327680 | tf_op jit(solution)/shard_map/all_to_all | solution.py:367
  192.4 0.0 copy-start
  192.4 3.1 %copy-done = bf16[128,2,2,7168]{3,2,1,0:T(2,128)(2,1)S(1)} copy-done((bf16[128,2,2,7168]{3,2,1,0:T(2,128)(2,1)S(1)}, bf16[128,2,2,7168]{3,2,1,0:T(2,128)(2,1)}, u32[]{:S(2)}) %copy-start) | copy-done | bytes 7340056
  195.5 6.5 %slot_dots.1 = f32[256,8]{1,0:T(8,128)S(1)} custom-call(bf16[28672,128]{1,0:T(8,128)(2,1)} %bitcast.21.got_ref, bf16[28672,128]{1,0:T(8,128)(2,1)S(1)} %bitcast.49), custom_call_target="tpu_custom_call" | custom-call | flops 8000000 | bytes 15000000 | tf_op jit(solution)/shard_map/slot_dots/pallas_call | solution.py:168
  202.0 0.1 copy.31
  202.1 0.5 reshape.103
  202.6 0.8 copy.32
  203.4 0.0 all-to-all-done.2
  203.4 9.4 %all-to-all-start.4 = ((f32[128,2,2]{1,2,0:T(2,128)}), f32[128,2,2]{1,2,0:T(2,128)S(1)}, u32[]{:S(2)}, u32[]{:S(2)}) async-start(f32[128,2,2]{1,2,0:T(2,128)} %copy.32), calls=%async_computation.4 | async-start | bytes 262144 | tf_op jit(solution)/shard_map/all_to_all | solution.py:371
  212.8 0.6 slice_bitcast_fusion.1
  213.5 0.6 reduce_sum.46
  214.1 8.6 %all-to-all-done.4 = f32[128,2,2]{1,2,0:T(2,128)S(1)} async-done(((f32[128,2,2]{1,2,0:T(2,128)}), f32[128,2,2]{1,2,0:T(2,128)S(1)}, u32[]{:S(2)}, u32[]{:S(2)}) %all-to-all-start.4) | async-done | bytes 2080 | tf_op jit(solution)/shard_map/all_to_all | solution.py:371
  222.7 0.9 copy.33
  223.6 0.2 reshape.104
  223.8 1.9 gather_fusion
  225.7 0.1 gather.7
  225.9 0.6 multiply_bitcast_fusion
  226.5 7.3 %copy.36 = bf16[128,2,2,7168]{3,2,1,0:T(2,128)(2,1)} copy(bf16[128,2,2,7168]{3,2,1,0:T(2,128)(2,1)} %all-to-all-done.3) | data formatting | bytes 14680064
  (7 shorter events, 0.1 us)
Async XLA Ops:
  0.6 28.2 %copy-start.5 = (f32[1,512]{1,0:T(1,128)S(1)}, f32[1,512]{1,0:T(1,128)}, u32[]{:S(2)}) copy-start(f32[1,512]{1,0:T(1,128)} %ratio_ref.3) | copy-start | bytes 6148
  0.6 28.2 %copy-start.6 = (s32[1,2]{1,0:T(1,128)S(1)}, s32[1,2]{1,0:T(1,128)}, u32[]{:S(2)}) copy-start(s32[1,2]{1,0:T(1,128)} %lengths_ref.3) | copy-start | bytes 28
  0.7 28.2 %copy-start.7 = (bf16[1,512,576]{1,2,0:T(8,128)(2,1)S(1)}, bf16[1,512,576]{1,2,0:T(8,128)(2,1)}, u32[]{:S(2)}) copy-start(bf16[1,512,576]{1,2,0:T(8,128)(2,1)} %param.14) | copy-start | bytes 1769476
  2.8 26.0 %all-to-all-start = ((bf16[16,64,576]{2,1,0:T(8,128)(2,1)}), bf16[16,64,576]{2,1,0:T(8,128)(2,1)S(1)}, u32[]{:S(2)}, u32[]{:S(2)}) async-start(bf16[16,64,576]{2,1,0:T(8,128)(2,1)} %broadcast_in_dim.23), calls=%async_computation | async-start | bytes 2621440 | tf_op jit(solution)/shard_map/all_to_all | solution.py:353
  58.3 4.4 %copy-start.2 = (bf16[1,32,7168]{2,1,0:T(8,128)(2,1)S(1)}, bf16[1,32,7168]{2,1,0:T(8,128)(2,1)}, u32[]{:S(2)}) copy-start(bf16[1,32,7168]{2,1,0:T(8,128)(2,1)} %param.18) | copy-start | bytes 1376260
  58.3 4.4 %copy-start.3 = (f32[1,32,8]{1,2,0:T(8,128)S(1)}, f32[1,32,8]{1,2,0:T(8,128)}, u32[]{:S(2)}) copy-start(f32[1,32,8]{1,2,0:T(8,128)} %param.20) | copy-start | bytes 3076
  58.3 4.4 %copy-start.4 = (s32[1,32,8]{1,2,0:T(8,128)S(1)}, s32[1,32,8]{1,2,0:T(8,128)}, u32[]{:S(2)}) copy-start(s32[1,32,8]{1,2,0:T(8,128)} %param.19) | copy-start | bytes 3076
  58.3 30.3 %all-to-all-start.1 = ((bf16[16,96,576]{2,1,0:T(8,128)(2,1)}), bf16[16,96,576]{2,1,0:T(8,128)(2,1)S(1)}, u32[]{:S(2)}, u32[]{:S(2)}) async-start(bf16[16,96,576]{2,1,0:T(8,128)(2,1)} %get-tuple-element.10), calls=%async_computation.1 | async-start | bytes 3932160 | tf_op jit(solution)/shard_map/all_to_all | solution.py:363
  67.6 3.1 %copy-start.1 = (bf16[28672,128]{1,0:T(8,128)(2,1)}, bf16[28672,128]{1,0:T(8,128)(2,1)S(1)}, u32[]{:S(2)}) copy-start(bf16[28672,128]{1,0:T(8,128)(2,1)S(1)} %get-tuple-element.11) | copy-start | bytes 22020100
  88.6 97.2 %all-to-all-start.3 = ((bf16[128,2,2,7168]{3,2,1,0:T(2,128)(2,1)}), bf16[128,2,2,7168]{3,2,1,0:T(2,128)(2,1)}, u32[]{:S(2)}, u32[]{:S(2)}) async-start(bf16[128,2,2,7168]{3,2,1,0:T(2,128)(2,1)} %bitcast.50), calls=%async_computation.3 | async-start | bytes 14680064 | tf_op jit(solution)/shard_map/all_to_all | solution.py:356
  185.8 17.5 %all-to-all-start.2 = ((f32[8,8,576]{2,1,0:T(8,128)}), f32[8,8,576]{2,1,0:T(8,128)S(1)}, u32[]{:S(2)}, u32[]{:S(2)}) async-start(f32[8,8,576]{2,1,0:T(8,128)} %slice_bitcast_fusion), calls=%async_computation.2 | async-start | bytes 327680 | tf_op jit(solution)/shard_map/all_to_all | solution.py:367
  192.4 3.1 %copy-start = (bf16[128,2,2,7168]{3,2,1,0:T(2,128)(2,1)S(1)}, bf16[128,2,2,7168]{3,2,1,0:T(2,128)(2,1)}, u32[]{:S(2)}) copy-start(bf16[128,2,2,7168]{3,2,1,0:T(2,128)(2,1)} %param.21) | copy-start | bytes 22020100
  203.4 19.3 %all-to-all-start.4 = ((f32[128,2,2]{1,2,0:T(2,128)}), f32[128,2,2]{1,2,0:T(2,128)S(1)}, u32[]{:S(2)}, u32[]{:S(2)}) async-start(f32[128,2,2]{1,2,0:T(2,128)} %copy.32), calls=%async_computation.4 | async-start | bytes 262144 | tf_op jit(solution)/shard_map/all_to_all | solution.py:371

commit v2 on v1

v2 whole, which is shorter than its diff:
```python
import jax
import jax.numpy as jnp
from jax import lax
from jax.experimental import pallas as pl
from jax.experimental.pallas import tpu as pltpu
from jax.sharding import PartitionSpec as P

EXPERTS = 256
CAP = 2
LANES = 128
PLACED = 4
VMEM = 58 << 20

score_scale = 192.0 ** (-0.5)
preference_beta = 0.5
route_scale = 2.5
log2_e = 1.4426950408889634

f32 = jnp.float32
bf16 = jnp.bfloat16


def coefficient_row(ratio_ref, lengths_ref, chosen_ref):
    rows = ratio_ref.shape[1]
    half = rows // 2
    lane = lax.broadcasted_iota(jnp.int32, (1, rows), 1)
    second = lane >= half
    position = jnp.where(second, lane - half, lane)
    length = jnp.where(second, lengths_ref[0, 1], lengths_ref[0, 0])
    live = position < length
    ratios = jnp.where(live, ratio_ref[...], 0.0)
    first_total = jnp.sum(jnp.where(second, 0.0, ratios), axis=1, keepdims=True)
    second_total = jnp.sum(jnp.where(second, ratios, 0.0), axis=1, keepdims=True)
    chosen = chosen_ref[0]
    margin = first_total - second_total
    margin = jnp.where(chosen == 0, margin, -margin)
    weight = preference_beta * jax.nn.sigmoid(-preference_beta * margin)
    signed = jnp.where(second == (chosen == 1), -weight, weight)
    return jnp.where(live, signed, 0.0)


def column_of(row):
    n = row.shape[1]
    return jnp.transpose(jnp.broadcast_to(row, (8, n)))[:, :1]


def router_gates(logits):
    affinity = jax.nn.sigmoid(logits)
    total = jnp.sum(affinity, axis=0, keepdims=True)
    return affinity, total, route_scale * affinity / total


def send_kernel(
    lengths_ref, chosen_ref, start_ref, ratio_ref, ids_ref, logits_ref, cot_ref,
    send_hbm, slot_ref, rows_ref, pair_ref, table_ref, gates_ref, table_smem, gates_smem, send_ref,
    sems, send_sems,
):
    tokens, model = cot_ref.shape
    top = ids_ref.shape[0]
    tiles = model // LANES
    parts = send_sems.shape[0]
    per_part = EXPERTS // parts
    part_rows = per_part * tiles * CAP

    _, _, gate = router_gates(logits_ref[...])
    gate = gate.astype(bf16).astype(f32)
    ids = jnp.transpose(ids_ref[...])
    gates = jnp.transpose(gate)
    expert = lax.broadcasted_iota(jnp.int32, (tokens, EXPERTS), 1)
    named = jnp.zeros((tokens, EXPERTS), f32)
    weight = jnp.zeros((tokens, EXPERTS), f32)
    for n in range(top):
        hit = ids[:, n : n + 1] == expert
        named = jnp.where(hit, 1.0, named)
        weight = jnp.where(hit, gates[:, n : n + 1], weight)
    row_i = lax.broadcasted_iota(jnp.int32, (tokens, tokens), 0)
    col_i = lax.broadcasted_iota(jnp.int32, (tokens, tokens), 1)
    before = jnp.dot(
        (col_i < row_i).astype(bf16), named.astype(bf16), preferred_element_type=f32
    )
    token = lax.broadcasted_iota(jnp.int32, (tokens, EXPERTS), 0).astype(f32)
    for s in range(CAP):
        here = jnp.where((before == float(s)) & (named > 0.0), 1.0, 0.0)
        table_ref[s : s + 1, :] = jnp.sum(here * token, axis=0, keepdims=True).astype(jnp.int32)
        gates_ref[s : s + 1, :] = jnp.sum(here * weight, axis=0, keepdims=True)
    table_copy = pltpu.make_async_copy(table_ref, table_smem, sems.at[0])
    gates_copy = pltpu.make_async_copy(gates_ref, gates_smem, sems.at[1])
    table_copy.start()
    gates_copy.start()
    slots = []
    for n in range(top):
        hit = ids[:, n : n + 1] == expert
        slots.append(jnp.sum(jnp.where(hit, before, 0.0), axis=1, keepdims=True))
    slot_ref[...] = jnp.transpose(jnp.concatenate(slots, axis=1)).astype(jnp.int32)
    coefficient = coefficient_row(ratio_ref, lengths_ref, chosen_ref)
    lane = lax.broadcasted_iota(jnp.int32, (tokens, coefficient.shape[1]), 1)
    row = lax.broadcasted_iota(jnp.int32, (tokens, coefficient.shape[1]), 0)
    own = jnp.sum(
        jnp.where(lane == row + start_ref[0], coefficient, 0.0), axis=1, keepdims=True
    )
    for tile in range(tiles):
        cot = cot_ref[:, tile * LANES : (tile + 1) * LANES].astype(f32)
        rows_ref[pl.ds(tile, tokens, stride=tiles), :] = (own * cot).astype(bf16).astype(f32)
    table_copy.wait()
    gates_copy.wait()

    def place(group, carry):
        for u in range(PLACED):
            e = group * PLACED + u
            for s in range(CAP):
                token = table_smem[s, e]
                block = rows_ref[pl.ds(pl.multiple_of(token * tiles, 8), tiles), :]
                pair_ref[u, pl.ds(s, tiles, stride=CAP), :] = block * gates_smem[s, e]
        for u in range(PLACED):
            at = pl.multiple_of((group * PLACED + u) * (tiles * CAP), 16)
            send_ref[pl.ds(at, tiles * CAP), :] = pair_ref[u].astype(bf16)
        return carry

    def send_copy(part):
        at = pl.ds(pl.multiple_of(part * part_rows, 16), part_rows)
        return pltpu.make_async_copy(send_ref.at[at], send_hbm.at[at], send_sems.at[part])

    def one_part(part, carry):
        first = part * (per_part // PLACED)
        lax.fori_loop(0, per_part // PLACED, lambda g, c: place(first + g, c), 0, unroll=2)
        send_copy(part).start()
        return carry

    lax.fori_loop(0, parts, one_part, 0)
    for part in range(parts):
        send_copy(part).wait()


def build_send(lengths, chosen, start, ratio, ids, logits, cot):
    tokens, model = cot.shape
    tiles = model // LANES
    rows = EXPERTS * CAP * tiles
    parts = 8
    smem = pl.BlockSpec(memory_space=pltpu.SMEM)
    vmem = pl.BlockSpec(memory_space=pltpu.VMEM)
    return pl.pallas_call(
        send_kernel,
        in_specs=[smem, smem, smem, vmem, vmem, vmem, vmem],
        out_specs=[pl.BlockSpec(memory_space=pl.ANY), vmem],
        out_shape=[
            jax.ShapeDtypeStruct((rows, LANES), bf16),
            jax.ShapeDtypeStruct(ids.shape, jnp.int32),
        ],
        scratch_shapes=[
            pltpu.VMEM((tokens * tiles, LANES), f32),
            pltpu.VMEM((PLACED, tiles * CAP, LANES), f32),
            pltpu.VMEM((8, EXPERTS), jnp.int32),
            pltpu.VMEM((8, EXPERTS), f32),
            pltpu.SMEM((8, EXPERTS), jnp.int32),
            pltpu.SMEM((8, EXPERTS), f32),
            pltpu.VMEM((rows, LANES), bf16),
            pltpu.SemaphoreType.DMA((2,)),
            pltpu.SemaphoreType.DMA((parts,)),
        ],
        compiler_params=pltpu.CompilerParams(vmem_limit_bytes=VMEM),
        cost_estimate=pl.CostEstimate(flops=0, bytes_accessed=8_000_000, transcendentals=0),
        name="build_send",
    )(lengths, chosen, start, ratio, ids, logits, cot)


def dot_kernel(got_hbm, saved_hbm, out_ref, rows_hbm, got_ref, saved_ref, acc_ref, sems):
    sources, wide = out_ref.shape
    per_owner = wide // 8
    parts = sems.shape[1]
    rows = got_ref.shape[0] // parts
    owners = sources // parts
    tall = rows // (owners * per_owner)

    def copies(part):
        at = pl.ds(pl.multiple_of(part * rows, 16), rows)
        return (
            pltpu.make_async_copy(got_hbm.at[at], got_ref.at[at], sems.at[0, part]),
            pltpu.make_async_copy(saved_hbm.at[at], saved_ref.at[at], sems.at[1, part]),
        )

    def pass_on(part):
        at = pl.ds(pl.multiple_of(part * rows, 16), rows)
        return pltpu.make_async_copy(got_ref.at[at], rows_hbm.at[at], sems.at[2, part])

    for part in range(parts):
        for copy in copies(part):
            copy.start()

    def work(part, carry):
        for copy in copies(part):
            copy.wait()
        pass_on(part).start()
        for p in range(owners * per_owner):
            at = pl.ds(pl.multiple_of(part * rows + p * tall, 16), tall)
            product = got_ref[at, :].astype(f32) * saved_ref[at, :].astype(f32)
            acc_ref[p] = jnp.sum(product.reshape(tall // 8, 8, LANES), axis=0)
        product = acc_ref[...].reshape(owners, per_owner, 8, LANES)
        out_ref[pl.ds(pl.multiple_of(part * owners, 8), owners), :] = jnp.concatenate(
            [jnp.sum(product[:, e], axis=2) for e in range(per_owner)], axis=1
        )
        return carry

    lax.fori_loop(0, parts, work, 0)
    for part in range(parts):
        pass_on(part).wait()


def slot_dots(got, saved, sources, per_owner):
    parts = 8
    anywhere = pl.BlockSpec(memory_space=pl.ANY)
    return pl.pallas_call(
        dot_kernel,
        in_specs=[anywhere, anywhere],
        out_specs=[pl.BlockSpec(memory_space=pltpu.VMEM), anywhere],
        out_shape=[
            jax.ShapeDtypeStruct((sources, per_owner * 8), f32),
            jax.ShapeDtypeStruct(got.shape, got.dtype),
        ],
        scratch_shapes=[
            pltpu.VMEM(got.shape, got.dtype),
            pltpu.VMEM(got.shape, got.dtype),
            pltpu.VMEM((sources // parts * per_owner, 8, LANES), f32),
            pltpu.SemaphoreType.DMA((3, parts)),
        ],
        compiler_params=pltpu.CompilerParams(vmem_limit_bytes=VMEM),
        cost_estimate=pl.CostEstimate(flops=8_000_000, bytes_accessed=15_000_000, transcendentals=0),
        name="slot_dots",
    )(got, saved)


def router_kernel(terms_ref, ids_ref, slot_ref, logits_ref, out_ref):
    top, tokens = ids_ref.shape
    owners, wide = terms_ref.shape
    per_owner = wide // 8
    affinity, total, gate = router_gates(logits_ref[...])
    ids = jnp.transpose(ids_ref[...])
    slots = jnp.transpose(slot_ref[...])
    terms = jnp.transpose(terms_ref[...])
    owner = lax.broadcasted_iota(jnp.int32, (tokens, owners), 1)
    columns = []
    for n in range(top):
        expert = ids[:, n : n + 1]
        slot = slots[:, n : n + 1]
        picked = jnp.zeros((tokens, owners), f32)
        for e in range(per_owner):
            for s in range(CAP):
                dot = jnp.zeros((1, owners), f32)
                for k in range(s, 8, CAP):
                    dot = dot + terms[e * 8 + k : e * 8 + k + 1]
                hit = (owner * per_owner + e == expert) & (slot == s)
                picked = jnp.where(hit, dot, picked)
        columns.append(jnp.sum(picked, axis=1, keepdims=True))
    gate_grad = jnp.transpose(jnp.concatenate(columns, axis=1)) / gate.astype(bf16).astype(f32)
    mixed = jnp.sum(gate_grad * affinity, axis=0, keepdims=True) / total
    out_ref[...] = route_scale / total * (gate_grad - mixed) * affinity * (1.0 - affinity)


def router_grad(terms, ids, slot, logits):
    return pl.pallas_call(
        router_kernel,
        out_shape=jax.ShapeDtypeStruct(logits.shape, f32),
        compiler_params=pltpu.CompilerParams(vmem_limit_bytes=VMEM),
        name="router_grad",
    )(terms, ids, slot, logits)


NT = (((1,), (1,)), ((), ()))


def attention_kernel(
    lengths_ref, chosen_ref, place_ref, ratio_ref, q_ref, cot_ref, prompt_ref, answer_ref,
    gq_ref, keep_ref, send_ref, keys_ref, keys_t_ref, acc_ref, value_ref,
):
    prompt_count, width = prompt_ref.shape
    row_count = answer_ref.shape[1]
    half = row_count // 2
    wide = keys_ref.shape[2]
    rank = value_ref.shape[1]
    pad = wide - width
    step = pl.program_id(0)

    @pl.when(step == 0)
    def _():
        answer_t = answer_ref[...]
        keys_t_ref[:, :prompt_count] = jnp.transpose(prompt_ref[...])
        keys_t_ref[:, prompt_count:] = answer_t
        latent = jnp.concatenate([prompt_ref[...], jnp.transpose(answer_t)], axis=0)
        zeros = jnp.zeros((latent.shape[0], pad), bf16)
        keys_ref[0] = jnp.concatenate([latent, zeros], axis=1)
        keys_ref[1] = jnp.concatenate([zeros, latent], axis=1)
        acc_ref[...] = jnp.zeros_like(acc_ref)
        value_ref[...] = jnp.zeros_like(value_ref)

    coefficient = column_of(coefficient_row(ratio_ref, lengths_ref, chosen_ref))
    key_i = lax.broadcasted_iota(jnp.int32, (half, half), 0)
    row_i = lax.broadcasted_iota(jnp.int32, (half, half), 1)
    causal = key_i <= row_i
    for k in range(2):
        rows = slice(k * half, (k + 1) * half)
        answer = slice(prompt_count + k * half, prompt_count + (k + 1) * half)
        grads = []
        for h in range(2):
            query = q_ref[rows, h * rank : h * rank + wide]
            grad_out = (
                coefficient[rows] * cot_ref[rows, h * rank : (h + 1) * rank].astype(f32)
            ).astype(bf16)
            s_prompt = lax.dot_general(
                keys_ref[h, :prompt_count], query, NT, preferred_element_type=f32
            )
            s_answer = lax.dot_general(keys_ref[h, answer], query, NT, preferred_element_type=f32)
            s_answer = jnp.where(causal, s_answer, -1e30)
            top = jnp.maximum(
                jnp.max(s_prompt, axis=0, keepdims=True), jnp.max(s_answer, axis=0, keepdims=True)
            )
            e_prompt = jnp.exp2((s_prompt - top) * (score_scale * log2_e))
            e_answer = jnp.exp2((s_answer - top) * (score_scale * log2_e))
            total = jnp.sum(e_prompt, axis=0, keepdims=True) + jnp.sum(
                e_answer, axis=0, keepdims=True
            )
            inverse = 1.0 / total
            p_prompt = e_prompt * inverse
            p_answer = e_answer * inverse
            b_prompt = p_prompt.astype(bf16)
            b_answer = p_answer.astype(bf16)
            d_prompt = lax.dot_general(
                keys_ref[0, :prompt_count, :rank], grad_out, NT, preferred_element_type=f32
            )
            d_answer = lax.dot_general(
                keys_ref[0, answer, :rank], grad_out, NT, preferred_element_type=f32
            )
            delta = jnp.sum(b_prompt.astype(f32) * d_prompt, axis=0, keepdims=True) + jnp.sum(
                b_answer.astype(f32) * d_answer, axis=0, keepdims=True
            )
            g_prompt = (p_prompt * (d_prompt - delta)).astype(bf16)
            g_answer = (p_answer * (d_answer - delta)).astype(bf16)
            grads.append(
                jnp.dot(keys_t_ref[:, :prompt_count], g_prompt, preferred_element_type=f32)
                + jnp.dot(keys_t_ref[:, answer], g_answer, preferred_element_type=f32)
            )
            acc_ref[h, :prompt_count] += jnp.dot(g_prompt, query, preferred_element_type=f32)
            acc_ref[h, answer] += jnp.dot(g_answer, query, preferred_element_type=f32)
            value_ref[:prompt_count] += jnp.dot(b_prompt, grad_out, preferred_element_type=f32)
            value_ref[answer] += jnp.dot(b_answer, grad_out, preferred_element_type=f32)
        both = (score_scale * jnp.concatenate(grads, axis=0)).astype(bf16)
        gq_ref[rows, :] = jnp.transpose(both)

    @pl.when(step == pl.num_programs(0) - 1)
    def _():
        half_chunks = send_ref.shape[0]
        prompt_rows = prompt_count // (2 * half_chunks)
        answer_rows = row_count // (2 * half_chunks)

        def combined(at):
            size = at.size
            key = acc_ref[0, at, :width] + pltpu.roll(acc_ref[1, at, :], wide - pad, 1)[:, :width]
            value = jnp.concatenate([value_ref[at, :], jnp.zeros((size, width - rank), f32)], axis=1)
            return (score_scale * key + value).astype(bf16)

        for side, out in enumerate((keep_ref, send_ref)):
            for c in range(half_chunks):
                chunk = side * half_chunks + c
                out[c, :prompt_rows] = combined(pl.ds(chunk * prompt_rows, prompt_rows))
                at = pl.multiple_of(prompt_count + place_ref[chunk] * answer_rows, answer_rows)
                out[c, prompt_rows:] = combined(pl.ds(at, answer_rows))


def attention(lengths, chosen, place, ratio, queries, cot, prompt, answer_t):
    rows, q_width = queries.shape
    prompt_count, width = prompt.shape
    heads = q_width // width
    rank = cot.shape[1] // heads
    wide = width + width - rank
    steps = heads // 2
    keys = prompt_count + rows
    chunks = place.shape[0]
    part = (chunks // 2, keys // chunks, width)
    whole = lambda shape: pl.BlockSpec(shape, lambda i: (0,) * len(shape))
    smem = pl.BlockSpec(memory_space=pltpu.SMEM)
    return pl.pallas_call(
        attention_kernel,
        grid=(steps,),
        in_specs=[
            smem, smem, smem, whole(ratio.shape),
            pl.BlockSpec((rows, 2 * width), lambda i: (0, i)),
            pl.BlockSpec((rows, 2 * rank), lambda i: (0, i)),
            whole(prompt.shape), whole(answer_t.shape),
        ],
        out_specs=[
            pl.BlockSpec((rows, 2 * width), lambda i: (0, i)),
            whole(part),
            whole(part),
        ],
        out_shape=[
            jax.ShapeDtypeStruct(queries.shape, bf16),
            jax.ShapeDtypeStruct(part, bf16),
            jax.ShapeDtypeStruct(part, bf16),
        ],
        scratch_shapes=[
            pltpu.VMEM((2, keys, wide), bf16),
            pltpu.VMEM((width, keys), bf16),
            pltpu.VMEM((2, keys, wide), f32),
            pltpu.VMEM((keys, rank), f32),
        ],
        compiler_params=pltpu.CompilerParams(vmem_limit_bytes=VMEM),
        cost_estimate=pl.CostEstimate(
            flops=17_000_000_000, bytes_accessed=9_000_000, transcendentals=2_600_000
        ),
        name="attention",
    )(lengths, chosen, place, ratio, queries, cot, prompt, answer_t)


def flat(x):
    n, e, s, d = x.shape
    t = d // LANES
    return x.reshape(n, e, s, t, LANES).transpose(0, 1, 3, 2, 4).reshape(n * e * t * s, LANES)


def unflat(x, n, e, s, d):
    t = d // LANES
    return x.reshape(n, e, t, s, LANES).transpose(0, 1, 3, 2, 4).reshape(n, e, s, d)


def ctx_moves(count, far, ring, core):
    rings = count // 4
    moves = []
    for f in range(2):
        for r in range(rings):
            for c in range(2):
                source = (f * rings + r) * 2 + c
                moves.append((source, ((f ^ far) * rings + (r + ring) % rings) * 2 + (c ^ core)))
    return moves


def resp_moves(count, ring, far):
    rings = count // 2
    return [
        (r * 2 + f, (r + ring) % rings * 2 + (f ^ far)) for r in range(rings) for f in range(2)
    ]


def gather_ring(latent, count):
    rings = count // 4
    return jnp.concatenate(
        [latent]
        + [lax.ppermute(latent, "ctx", ctx_moves(count, 0, rings - d, 0)) for d in range(1, rings)]
    )


def ctx_places(count):
    rings = count // 4
    me = lax.axis_index("ctx")
    order = jnp.arange(count, dtype=jnp.int32)
    core, far, ring = order // (rings * 2), order // rings % 2, order % rings
    my_core, my_ring, my_far = me % 2, me // 2 % rings, me // (rings * 2)
    return ((my_far ^ far) * rings + (my_ring + ring) % rings) * 2 + (my_core ^ core)


def reduce_over_cores(keep, send, count):
    got = lax.ppermute(send, "ctx", ctx_moves(count, 0, 0, 1))
    return (keep.astype(f32) + got.astype(f32)).reshape((2, count // 4) + keep.shape[1:])


def both_moves(ctx_count, resp_count):
    return [
        (c0 * resp_count + r0, c1 * resp_count + r1)
        for c0, c1 in ctx_moves(ctx_count, 1, 0, 0)
        for r0, r1 in resp_moves(resp_count, 0, 1)
    ]


def reduce_over_ring(held, count):
    low = held.astype(bf16)
    mine = held[:, 0]
    for d in range(1, count // 4):
        mine = mine + lax.ppermute(low[:, d], "ctx", ctx_moves(count, 0, d, 0)).astype(f32)
    return mine


def reduce_answer(rows, count):
    return rows[0] + lax.ppermute(rows[1], "ctx", ctx_moves(count, 1, 0, 0))


def reduce_prompt(rows, ctx_count, resp_count):
    rings = resp_count // 2
    me = lax.axis_index("resp")
    my_ring, my_far = me // 2, me % 2
    blocks = rows.reshape(2, rings, 2, rows.shape[1] // resp_count, rows.shape[2])
    twice = jnp.concatenate([blocks, blocks[:, : rings - 1]], axis=1)
    blocks = lax.dynamic_slice_in_dim(twice, my_ring, rings, axis=1)
    mine = blocks[:, 0]
    for d in range(1, rings):
        mine = mine + lax.ppermute(blocks[:, d], "resp", resp_moves(resp_count, d, 0))
    own = lax.dynamic_index_in_dim(mine, my_far, axis=1, keepdims=False)
    others = lax.dynamic_index_in_dim(mine, 1 - my_far, axis=1, keepdims=False)
    return (
        own[0]
        + lax.ppermute(own[1], "ctx", ctx_moves(ctx_count, 1, 0, 0))
        + lax.ppermute(others[0], "resp", resp_moves(resp_count, 0, 1))
        + lax.ppermute(others[1], ("ctx", "resp"), both_moves(ctx_count, resp_count))
    )


def on_device(
    queries,
    attn_cot,
    prompt_latent,
    response_latent,
    log_ratio,
    lengths,
    chosen,
    moe_cot,
    expert_ids,
    router_logits,
    expert_outputs,
):
    ctx_count = lax.axis_size("ctx")
    resp_count = lax.axis_size("resp")
    devices = ctx_count * resp_count
    width = prompt_latent.shape[1]
    tokens, model = moe_cot.shape[1:]
    per_owner = EXPERTS // devices
    start = (lax.axis_index("ctx") * tokens).astype(jnp.int32).reshape(1)
    ids = expert_ids[0].T
    logits = router_logits[0].T

    ring = gather_ring(prompt_latent, ctx_count)
    ring, cot = lax.optimization_barrier((ring, moe_cot[0]))
    sent, slot = build_send(lengths, chosen, start, log_ratio, ids, logits, cot)
    far = lax.ppermute(ring, "ctx", ctx_moves(ctx_count, 1, 0, 0))
    sent, around = lax.optimization_barrier((sent, jnp.concatenate([ring, far])))
    other = lax.ppermute(around, "ctx", ctx_moves(ctx_count, 0, 0, 1))
    arrived = lax.all_to_all(
        unflat(sent, devices, per_owner, CAP, model), ("ctx", "resp"), 0, 0, tiled=True
    )

    grad_query, keep, send = attention(
        lengths, chosen, ctx_places(ctx_count), log_ratio, queries[0], attn_cot[0],
        jnp.concatenate([around, other]), response_latent[0].T,
    )
    held = reduce_over_cores(keep, send, ctx_count)
    terms, rows = slot_dots(flat(arrived), flat(expert_outputs), devices, per_owner)
    mine = reduce_over_ring(held, ctx_count)
    mine, terms = lax.optimization_barrier((mine, terms))
    returned = lax.all_to_all(terms, ("ctx", "resp"), 0, 0, tiled=True)
    prompt_rows = prompt_latent.shape[0]
    grad_response = reduce_answer(mine[:, prompt_rows:], ctx_count)[None]
    grad_prompt = reduce_prompt(mine[:, :prompt_rows], ctx_count, resp_count)

    returned, grad_prompt, grad_response = lax.optimization_barrier(
        (returned, grad_prompt, grad_response)
    )
    grad_router = router_grad(returned, ids, slot, logits)
    expert_row_grads = unflat(rows, devices, per_owner, CAP, model)
    return (grad_query[None], grad_prompt, grad_response, expert_row_grads, grad_router.T[None])


def solution(mesh):
    placed = (
        P("resp", None, "ctx"),
        P("resp", None, "ctx"),
        P("ctx", None),
        P("resp", None, None),
        P("resp", None),
        P("resp", None),
        P("resp"),
        P("resp", "ctx", None),
        P("resp", "ctx", None),
        P("resp", "ctx", None),
        P(None, ("ctx", "resp"), None, None),
    )
    return jax.shard_map(
        on_device,
        mesh=mesh,
        in_specs=placed,
        out_specs=(
            P("resp", None, "ctx"),
            P(("ctx", "resp"), None),
            P("resp", "ctx", None),
            P(None, ("ctx", "resp"), None, None),
            P("resp", "ctx", None),
        ),
        check_vma=False,
    )
```

time: 234 us -> 165 us (0.71)
  waiting for transfers between devices: 131 us -> 62.6 us
  local copies, waits for them, and re-layouts: 21.4 us -> 1.34 us
  Pallas kernels: 40.8 us -> 48.3 us
  starting transfers between devices: 37.5 us -> 44.8 us
  other arithmetic: 1.68 us -> 5.64 us
    all_to_all x1, waiting for transfers between devices: 86.4 us -> 0.01 us  [on_device(): lax.all_to_all(unflat(sent, devices, per_owner, CAP, model), ('ctx', 'res...]
    ppermute x0 -> x16, waiting for transfers between devices: none -> 62.6 us  [the longest x3 52.2 us: reduce_over_ring(): lax.ppermute(low[:, d], 'ctx', ctx_moves(count, 0, d, 0)).astype(f32)]
    all_to_all x4 -> x1, waiting for transfers between devices: 44.6 us -> 0.01 us  [on_device(): returned = lax.all_to_all(terms, ('ctx', 'resp'), 0, 0, tiled=True)]
    ppermute x0 -> x16, starting transfers between devices: none -> 25.2 us  [the longest x3 7.36 us: reduce_prompt(): lax.ppermute(blocks[:, d], 'resp', resp_moves(resp_count, d, 0))]
    all_to_all x4 -> x1, starting transfers between devices: 27.7 us -> 8.87 us  [on_device(): returned = lax.all_to_all(terms, ('ctx', 'resp'), 0, 0, tiled=True)]
    unnamed x17 -> x3, local copies, waits for them, and re-layouts: 13.4 us -> 0.65 us
    pallas_call x3 -> x4, Pallas kernels: 40.8 us -> 48.3 us  [the longest x1 30.6 us: attention(): pl.pallas_call(attention_kernel, grid=(steps,), in_specs=[smem, smem, sme...]
    broadcast_in_dim x2 -> x0, local copies, waits for them, and re-layouts: 2.8 us -> none  [the longest x1 2.16 us: on_device(): jnp.broadcast_to(prompt_latent[None], (ctx_count,) + prompt_latent.shape)]
  transfers between devices with their start and end apart: 5 -> 18, of which waited for: 4 -> 8; matrix products, arithmetic and copies ran while one was open for 2% -> 3% of each run, Pallas kernels for 5% -> 22%
where the time goes in v2:
time: 165 us; the launch traced here: 164 us
  waiting for transfers between devices  62.6 us (38%)
  Pallas kernels  48.3 us (29%)
  starting transfers between devices  44.8 us (27%)
  other arithmetic  5.64 us (3%)
    ppermute x3, waiting for transfers between devices, reduce_over_ring(): lax.ppermute(low[:, d], 'ctx', ctx_moves(count, 0, d, 0)).astype(f32)  52.2 us
    pallas_call x1, Pallas kernels, attention(): pl.pallas_call(attention_kernel, grid=(steps,), in_specs=[smem, smem, sme...  30.6 us
    all_to_all x1, starting transfers between devices, on_device(): lax.all_to_all(unflat(sent, devices, per_owner, CAP, model), ('ctx', 'res...  10.7 us
    pallas_call x1, Pallas kernels, slot_dots(): pl.pallas_call(dot_kernel, in_specs=[anywhere, anywhere], out_specs=[pl.B...  9.12 us
    all_to_all x1, starting transfers between devices, on_device(): returned = lax.all_to_all(terms, ('ctx', 'resp'), 0, 0, tiled=True)  8.87 us
    ppermute x3, starting transfers between devices, reduce_prompt(): lax.ppermute(blocks[:, d], 'resp', resp_moves(resp_count, d, 0))  7.36 us
    pallas_call x1, Pallas kernels, build_send(): pl.pallas_call(send_kernel, in_specs=[smem, smem, smem, vmem, vmem, vmem,...  6.28 us
    ppermute x3, starting transfers between devices, gather_ring(): lax.ppermute(latent, 'ctx', ctx_moves(count, 0, rings - d, 0))  5.29 us
  transfers between devices with their start and end apart: 18, of which 8 were waited for; matrix products, arithmetic and copies ran while one was open for 3% of the time, Pallas kernels for 22%

profile of v2, /device:TPU:1, one launch (start us, length us, event | category | flops | bytes accessed | tf_op | source)
XLA Modules:
  0.0 164.1 jit_solution(9290217774707924065)
XLA Ops:
  0.6 3.8 %collective-permute-start.1 = (bf16[64,576]{1,0:T(8,128)(2,1)}, bf16[64,576]{1,0:T(8,128)(2,1)S(1)}, u32[]{:S(2)}, u32[]{:S(2)}) collective-permute-start(bf16[64,576]{1,0:T(8,128)(2,1)} %param.13), channel_id=1, source_target_pairs={{0,32},{8,40},{16,48},{24,56},{32,0},{40,8},{48,16},{56,24},{64,96... | collective-permute-start | bytes 221192 | tf_op jit(solution)/shard_map/ppermute | solution.py:445
  4.5 0.8 collective-permute-start
  5.2 0.7 collective-permute-start.2
  5.9 0.6 collective-permute-done.1
  6.5 2.3 %collective-permute-done = bf16[64,576]{1,0:T(8,128)(2,1)S(1)} collective-permute-done((bf16[64,576]{1,0:T(8,128)(2,1)}, bf16[64,576]{1,0:T(8,128)(2,1)S(1)}, u32[]{:S(2)}, u32[]{:S(2)}) %collective-permute-start) | collective-permute-done | bytes 73760 | tf_op jit(solution)/shard_map/ppermute | solution.py:445
  8.8 1.2 collective-permute-done.2
  9.9 0.9 pad_maximum_fusion.2
  10.9 1.7 %collective-permute-start.3 = (bf16[256,576]{1,0:T(8,128)(2,1)S(1)}, bf16[256,576]{1,0:T(8,128)(2,1)S(1)}, u32[]{:S(2)}, u32[]{:S(2)}) collective-permute-start(bf16[256,576]{1,0:T(8,128)(2,1)S(1)} %pad_maximum_fusion.2), channel_id=1, source_target_pairs={{0,64},{8,72},{16,80},{24,88},{32,96},{40,104},{48,112},{56,120},{... | collective-permute-start | bytes 884744 | tf_op jit(solution)/shard_map/ppermute | solution.py:529
  13.2 6.3 %build_send.1 = (bf16[28672,128]{1,0:T(8,128)(2,1)}, s32[8,32]{1,0:T(8,128)}) custom-call(s32[1,2]{1,0:T(1,128)} %lengths_ref.3, s32[1]{0:T(128)S(6)} %copy.40.chosen_ref, s32[1]{0:T(128)} %bitcast.2.start_ref, f32[1,512]{1,0:T(1,128)} %ratio_ref.3, s32[8,32]{1,0:T(8,128)} %bitcast.101, f32[8,32]{1,0:T(8,128)} %bitcast.103, bf16[32,7168]{1,0:T(8,128)(2,1)} %bitcast.99), custom_call_target="tpu_custom_call" | custom-call | bytes 8000000 | tf_op jit(solution)/shard_map/build_send/pallas_call | solution.py:141
  19.5 0.0 collective-permute-done.3
  19.5 0.1 pad_maximum_fusion.1
  19.6 10.7 %all-to-all-start = ((bf16[128,2,2,7168]{3,2,1,0:T(2,128)(2,1)}), bf16[128,2,2,7168]{3,2,1,0:T(2,128)(2,1)}, u32[]{:S(2)}, u32[]{:S(2)}) async-start(bf16[128,2,2,7168]{3,2,1,0:T(2,128)(2,1)} %bitcast.94), calls=%async_computation | async-start | bytes 14680064 | tf_op jit(solution)/shard_map/all_to_all | solution.py:532
  30.3 0.2 copy.22
  30.5 1.2 collective-permute-start.4
  31.8 0.5 fusion.14.place_ref
  32.3 1.1 collective-permute-done.4
  33.4 0.3 copy.23
  33.7 1.3 pad_maximum_fusion.prompt_ref
  35.0 30.6 %attention.1 = (bf16[512,2304]{1,0:T(8,128)(2,1)}, bf16[8,96,576]{2,1,0:T(8,128)(2,1)}, bf16[8,96,576]{2,1,0:T(8,128)(2,1)}) custom-call(s32[1,2]{1,0:T(1,128)} %lengths_ref.3, s32[1]{0:T(128)S(6)} %copy.40.chosen_ref, s32[16]{0:T(128)} %fusion.14.place_ref, f32[1,512]{1,0:T(1,128)} %ratio_ref.3, bf16[512,2304]{1,0:T(8,128)(2,1)} %bitcast.107, ...), custom_call_target="tpu_custom_call" | custom-call | flops 16999999488 | bytes 9000000 | tf_op jit(solution)/shard_map/attention/pallas_call | solution.py:379
  65.6 0.4 collective-permute-start.5
  66.0 2.4 %collective-permute-done.5 = bf16[8,96,576]{2,1,0:T(8,128)(2,1)S(1)} collective-permute-done((bf16[8,96,576]{2,1,0:T(8,128)(2,1)}, bf16[8,96,576]{2,1,0:T(8,128)(2,1)S(1)}, u32[]{:S(2)}, u32[]{:S(2)}) %collective-permute-start.5) | collective-permute-done | bytes 884768 | tf_op jit(solution)/shard_map/ppermute | solution.py:459
  68.4 1.4 convert_add_fusion
  69.8 0.1 slice_bitcast_fusion.3
  69.9 0.7 collective-permute-start.6
  70.6 2.0 %collective-permute-start.8 = (bf16[2,96,576]{2,1,0:T(8,128)(2,1)S(1)}, bf16[2,96,576]{2,1,0:T(8,128)(2,1)S(1)}, u32[]{:S(2)}, u32[]{:S(2)}) collective-permute-start(bf16[2,96,576]{2,1,0:T(8,128)(2,1)S(1)} %get-tuple-element.38), channel_id=1, source_target_pairs={{0,48},{8,56},{16,0},{24,8},{32,16},{40,24},{48,32},{56,40},{64,11... | collective-permute-start | bytes 663560 | tf_op jit(solution)/shard_map/ppermute | solution.py:475
  72.7 0.9 collective-permute-start.7
  73.6 52.1 %collective-permute-done.6 = bf16[2,96,576]{2,1,0:T(8,128)(2,1)S(1)} collective-permute-done((bf16[2,96,576]{2,1,0:T(8,128)(2,1)S(1)}, bf16[2,96,576]{2,1,0:T(8,128)(2,1)S(1)}, u32[]{:S(2)}, u32[]{:S(2)}) %collective-permute-start.6) | collective-permute-done | bytes 221216 | tf_op jit(solution)/shard_map/ppermute | solution.py:475
  125.7 0.0 collective-permute-done.8
  125.8 0.0 collective-permute-done.7
  125.8 0.1 fusion.2
  125.9 0.0 all-to-all-done
  125.9 9.1 %slot_dots.1 = (f32[128,16]{1,0:T(8,128)}, bf16[28672,128]{1,0:T(8,128)(2,1)}) custom-call(bf16[28672,128]{1,0:T(8,128)(2,1)} %bitcast.21.got_hbm, bf16[28672,128]{1,0:T(8,128)(2,1)} %bitcast.93), custom_call_target="tpu_custom_call" | custom-call | flops 8000000 | bytes 15000000 | tf_op jit(solution)/shard_map/slot_dots/pallas_call | solution.py:211
  135.1 0.1 fusion.3
  135.2 1.4 collective-permute-start.9
  136.6 4.0 %collective-permute-start.10 = (f32[2,2,8,576]{3,2,1,0:T(8,128)S(1)}, f32[2,2,8,576]{3,2,1,0:T(8,128)S(1)}, u32[]{:S(2)}, u32[]{:S(2)}) collective-permute-start(f32[2,2,8,576]{3,2,1,0:T(8,128)S(1)} %get-tuple-element.41), channel_id=1, source_target_pairs={{0,4},{1,5},{2,6},{3,7},{4,0},{5,1},{6,2},{7,3},{8,12},{9,13},{10,... | collective-permute-start | bytes 221192 | tf_op jit(solution)/shard_map/ppermute | solution.py:492
  140.6 2.0 %collective-permute-start.11 = (f32[2,2,8,576]{3,2,1,0:T(8,128)S(1)}, f32[2,2,8,576]{3,2,1,0:T(8,128)S(1)}, u32[]{:S(2)}, u32[]{:S(2)}) collective-permute-start(f32[2,2,8,576]{3,2,1,0:T(8,128)S(1)} %get-tuple-element.42), channel_id=1, source_target_pairs={{0,6},{1,7},{2,0},{3,1},{4,2},{5,3},{6,4},{7,5},{8,14},{9,15},{10,... | collective-permute-start | bytes 221192 | tf_op jit(solution)/shard_map/ppermute | solution.py:492
  142.6 8.9 %all-to-all-start.1 = ((f32[128,1,16]{2,1,0:T(1,128)}), f32[128,1,16]{2,1,0:T(1,128)S(1)}, u32[]{:S(2)}, u32[]{:S(2)}) async-start(f32[128,1,16]{2,1,0:T(1,128)} %bitcast.26), calls=%async_computation.1 | async-start | bytes 131072 | tf_op jit(solution)/shard_map/all_to_all | solution.py:544
  151.4 1.6 collective-permute-start.15
  153.0 0.0 collective-permute-done.9
  153.0 0.0 collective-permute-done.10
  153.0 0.0 collective-permute-done.11
  153.1 0.1 collective-permute-start.12
  153.2 3.2 %collective-permute-start.13 = (f32[8,576]{1,0:T(8,128)S(1)}, f32[8,576]{1,0:T(8,128)S(1)}, u32[]{:S(2)}, u32[]{:S(2)}) collective-permute-start(f32[8,576]{1,0:T(8,128)S(1)} %get-tuple-element.44), channel_id=1, source_target_pairs={{0,1},{1,0},{2,3},{3,2},{4,5},{5,4},{6,7},{7,6},{8,9},{9,8},{10,11... | collective-permute-start | bytes 55304 | tf_op jit(solution)/shard_map/ppermute | solution.py:498
  156.4 0.6 collective-permute-start.14
  157.0 0.0 collective-permute-done.15
  157.0 0.6 fusion.7
  157.7 0.0 collective-permute-done.12
  157.7 1.8 %collective-permute-done.13 = f32[8,576]{1,0:T(8,128)S(1)} collective-permute-done((f32[8,576]{1,0:T(8,128)S(1)}, f32[8,576]{1,0:T(8,128)S(1)}, u32[]{:S(2)}, u32[]{:S(2)}) %collective-permute-start.13) | collective-permute-done | bytes 18464 | tf_op jit(solution)/shard_map/ppermute | solution.py:498
  159.5 1.1 collective-permute-done.14
  160.6 0.6 fusion.10
  161.2 0.0 all-to-all-done.1
  161.2 0.0 copy-start
  161.2 0.6 copy-done
  161.8 2.3 %router_grad.1 = f32[8,32]{1,0:T(8,128)} custom-call(f32[128,16]{1,0:T(8,128)} %bitcast.100, s32[8,32]{1,0:T(8,128)} %bitcast.102, s32[8,32]{1,0:T(8,128)} %get-tuple-element.36.slot_ref, f32[8,32]{1,0:T(8,128)} %bitcast.104), custom_call_target="tpu_custom_call" | custom-call | tf_op jit(solution)/shard_map/router_grad/pallas_call | solution.py:259
  (7 shorter events, 0.1 us)
Async XLA Ops:
  0.6 5.9 %collective-permute-start.1 = (bf16[64,576]{1,0:T(8,128)(2,1)}, bf16[64,576]{1,0:T(8,128)(2,1)S(1)}, u32[]{:S(2)}, u32[]{:S(2)}) collective-permute-start(bf16[64,576]{1,0:T(8,128)(2,1)} %param.13), channel_id=1, source_target_pairs={{0,32},{8,40},{16,48},{24,56},{32,0},{40,8},{48,16},{56,24},{64,96... | collective-permute-start | bytes 221192 | tf_op jit(solution)/shard_map/ppermute | solution.py:445
  4.5 4.3 %collective-permute-start = (bf16[64,576]{1,0:T(8,128)(2,1)}, bf16[64,576]{1,0:T(8,128)(2,1)S(1)}, u32[]{:S(2)}, u32[]{:S(2)}) collective-permute-start(bf16[64,576]{1,0:T(8,128)(2,1)} %param.13), channel_id=1, source_target_pairs={{0,48},{8,56},{16,0},{24,8},{32,16},{40,24},{48,32},{56,40},{64,11... | collective-permute-start | bytes 221192 | tf_op jit(solution)/shard_map/ppermute | solution.py:445
  5.2 4.7 %collective-permute-start.2 = (bf16[64,576]{1,0:T(8,128)(2,1)}, bf16[64,576]{1,0:T(8,128)(2,1)S(1)}, u32[]{:S(2)}, u32[]{:S(2)}) collective-permute-start(bf16[64,576]{1,0:T(8,128)(2,1)} %param.13), channel_id=1, source_target_pairs={{0,16},{8,24},{16,32},{24,40},{32,48},{40,56},{48,0},{56,8},{64,80... | collective-permute-start | bytes 221192 | tf_op jit(solution)/shard_map/ppermute | solution.py:445
  10.9 8.7 %collective-permute-start.3 = (bf16[256,576]{1,0:T(8,128)(2,1)S(1)}, bf16[256,576]{1,0:T(8,128)(2,1)S(1)}, u32[]{:S(2)}, u32[]{:S(2)}) collective-permute-start(bf16[256,576]{1,0:T(8,128)(2,1)S(1)} %pad_maximum_fusion.2), channel_id=1, source_target_pairs={{0,64},{8,72},{16,80},{24,88},{32,96},{40,104},{48,112},{56,120},{... | collective-permute-start | bytes 884744 | tf_op jit(solution)/shard_map/ppermute | solution.py:529
  19.6 106.3 %all-to-all-start = ((bf16[128,2,2,7168]{3,2,1,0:T(2,128)(2,1)}), bf16[128,2,2,7168]{3,2,1,0:T(2,128)(2,1)}, u32[]{:S(2)}, u32[]{:S(2)}) async-start(bf16[128,2,2,7168]{3,2,1,0:T(2,128)(2,1)} %bitcast.94), calls=%async_computation | async-start | bytes 14680064 | tf_op jit(solution)/shard_map/all_to_all | solution.py:532
  30.5 2.8 %collective-permute-start.4 = (bf16[512,576]{0,1:T(8,128)(2,1)S(1)}, bf16[512,576]{0,1:T(8,128)(2,1)S(1)}, u32[]{:S(2)}, u32[]{:S(2)}) collective-permute-start(bf16[512,576]{0,1:T(8,128)(2,1)S(1)} %copy.22), channel_id=1, source_target_pairs={{0,8},{8,0},{16,24},{24,16},{32,40},{40,32},{48,56},{56,48},{64,72... | collective-permute-start | bytes 1769480 | tf_op jit(solution)/shard_map/ppermute | solution.py:531
  65.6 2.9 %collective-permute-start.5 = (bf16[8,96,576]{2,1,0:T(8,128)(2,1)}, bf16[8,96,576]{2,1,0:T(8,128)(2,1)S(1)}, u32[]{:S(2)}, u32[]{:S(2)}) collective-permute-start(bf16[8,96,576]{2,1,0:T(8,128)(2,1)} %get-tuple-element.27), channel_id=1, source_target_pairs={{0,8},{8,0},{16,24},{24,16},{32,40},{40,32},{48,56},{56,48},{64,72... | collective-permute-start | bytes 2654216 | tf_op jit(solution)/shard_map/ppermute | solution.py:459
  69.9 55.8 %collective-permute-start.6 = (bf16[2,96,576]{2,1,0:T(8,128)(2,1)S(1)}, bf16[2,96,576]{2,1,0:T(8,128)(2,1)S(1)}, u32[]{:S(2)}, u32[]{:S(2)}) collective-permute-start(bf16[2,96,576]{2,1,0:T(8,128)(2,1)S(1)} %get-tuple-element.37), channel_id=1, source_target_pairs={{0,16},{8,24},{16,32},{24,40},{32,48},{40,56},{48,0},{56,8},{64,80... | collective-permute-start | bytes 663560 | tf_op jit(solution)/shard_map/ppermute | solution.py:475
  70.6 55.1 %collective-permute-start.8 = (bf16[2,96,576]{2,1,0:T(8,128)(2,1)S(1)}, bf16[2,96,576]{2,1,0:T(8,128)(2,1)S(1)}, u32[]{:S(2)}, u32[]{:S(2)}) collective-permute-start(bf16[2,96,576]{2,1,0:T(8,128)(2,1)S(1)} %get-tuple-element.38), channel_id=1, source_target_pairs={{0,48},{8,56},{16,0},{24,8},{32,16},{40,24},{48,32},{56,40},{64,11... | collective-permute-start | bytes 663560 | tf_op jit(solution)/shard_map/ppermute | solution.py:475
  72.7 53.1 %collective-permute-start.7 = (bf16[2,96,576]{2,1,0:T(8,128)(2,1)S(1)}, bf16[2,96,576]{2,1,0:T(8,128)(2,1)S(1)}, u32[]{:S(2)}, u32[]{:S(2)}) collective-permute-start(bf16[2,96,576]{2,1,0:T(8,128)(2,1)S(1)} %get-tuple-element.39), channel_id=1, source_target_pairs={{0,32},{8,40},{16,48},{24,56},{32,0},{40,8},{48,16},{56,24},{64,96... | collective-permute-start | bytes 663560 | tf_op jit(solution)/shard_map/ppermute | solution.py:475
  135.2 17.8 %collective-permute-start.9 = (f32[2,2,8,576]{3,2,1,0:T(8,128)S(1)}, f32[2,2,8,576]{3,2,1,0:T(8,128)S(1)}, u32[]{:S(2)}, u32[]{:S(2)}) collective-permute-start(f32[2,2,8,576]{3,2,1,0:T(8,128)S(1)} %get-tuple-element.40), channel_id=1, source_target_pairs={{0,2},{1,3},{2,4},{3,5},{4,6},{5,7},{6,0},{7,1},{8,10},{9,11},{10,... | collective-permute-start | bytes 221192 | tf_op jit(solution)/shard_map/ppermute | solution.py:492
  136.6 16.4 %collective-permute-start.10 = (f32[2,2,8,576]{3,2,1,0:T(8,128)S(1)}, f32[2,2,8,576]{3,2,1,0:T(8,128)S(1)}, u32[]{:S(2)}, u32[]{:S(2)}) collective-permute-start(f32[2,2,8,576]{3,2,1,0:T(8,128)S(1)} %get-tuple-element.41), channel_id=1, source_target_pairs={{0,4},{1,5},{2,6},{3,7},{4,0},{5,1},{6,2},{7,3},{8,12},{9,13},{10,... | collective-permute-start | bytes 221192 | tf_op jit(solution)/shard_map/ppermute | solution.py:492
  140.6 12.5 %collective-permute-start.11 = (f32[2,2,8,576]{3,2,1,0:T(8,128)S(1)}, f32[2,2,8,576]{3,2,1,0:T(8,128)S(1)}, u32[]{:S(2)}, u32[]{:S(2)}) collective-permute-start(f32[2,2,8,576]{3,2,1,0:T(8,128)S(1)} %get-tuple-element.42), channel_id=1, source_target_pairs={{0,6},{1,7},{2,0},{3,1},{4,2},{5,3},{6,4},{7,5},{8,14},{9,15},{10,... | collective-permute-start | bytes 221192 | tf_op jit(solution)/shard_map/ppermute | solution.py:492
  142.6 18.7 %all-to-all-start.1 = ((f32[128,1,16]{2,1,0:T(1,128)}), f32[128,1,16]{2,1,0:T(1,128)S(1)}, u32[]{:S(2)}, u32[]{:S(2)}) async-start(f32[128,1,16]{2,1,0:T(1,128)} %bitcast.26), calls=%async_computation.1 | async-start | bytes 131072 | tf_op jit(solution)/shard_map/all_to_all | solution.py:544
  151.4 5.6 %collective-permute-start.15 = (f32[32,576]{1,0:T(8,128)S(1)}, f32[32,576]{1,0:T(8,128)S(1)}, u32[]{:S(2)}, u32[]{:S(2)}) collective-permute-start(f32[32,576]{1,0:T(8,128)S(1)} %slice_bitcast_fusion.8), channel_id=1, source_target_pairs={{0,64},{8,72},{16,80},{24,88},{32,96},{40,104},{48,112},{56,120},{... | collective-permute-start | bytes 221192 | tf_op jit(solution)/shard_map/ppermute | solution.py:480
  153.1 4.6 %collective-permute-start.12 = (f32[8,576]{1,0:T(8,128)S(1)}, f32[8,576]{1,0:T(8,128)S(1)}, u32[]{:S(2)}, u32[]{:S(2)}) collective-permute-start(f32[8,576]{1,0:T(8,128)S(1)} %get-tuple-element.43), channel_id=1, source_target_pairs={{0,64},{8,72},{16,80},{24,88},{32,96},{40,104},{48,112},{56,120},{... | collective-permute-start | bytes 55304 | tf_op jit(solution)/shard_map/ppermute | solution.py:497
  153.2 6.3 %collective-permute-start.13 = (f32[8,576]{1,0:T(8,128)S(1)}, f32[8,576]{1,0:T(8,128)S(1)}, u32[]{:S(2)}, u32[]{:S(2)}) collective-permute-start(f32[8,576]{1,0:T(8,128)S(1)} %get-tuple-element.44), channel_id=1, source_target_pairs={{0,1},{1,0},{2,3},{3,2},{4,5},{5,4},{6,7},{7,6},{8,9},{9,8},{10,11... | collective-permute-start | bytes 55304 | tf_op jit(solution)/shard_map/ppermute | solution.py:498
  156.4 4.2 %collective-permute-start.14 = (f32[8,576]{1,0:T(8,128)S(1)}, f32[8,576]{1,0:T(8,128)S(1)}, u32[]{:S(2)}, u32[]{:S(2)}) collective-permute-start(f32[8,576]{1,0:T(8,128)S(1)} %get-tuple-element.45), channel_id=1, source_target_pairs={{0,65},{1,64},{2,67},{3,66},{4,69},{5,68},{6,71},{7,70},{8,73},{9,... | collective-permute-start | bytes 55304 | tf_op jit(solution)/shard_map/ppermute | solution.py:499
  161.2 0.6 copy-start

commit v3 on v2

--- a/solution.py
+++ b/solution.py
@@ -50,18 +50,13 @@
     return affinity, total, route_scale * affinity / total
 
 
-def send_kernel(
+def plan_kernel(
     lengths_ref, chosen_ref, start_ref, ratio_ref, ids_ref, logits_ref, cot_ref,
-    send_hbm, slot_ref, rows_ref, pair_ref, table_ref, gates_ref, table_smem, gates_smem, send_ref,
-    sems, send_sems,
+    rows_ref, slot_ref, table_ref, gates_ref,
 ):
     tokens, model = cot_ref.shape
     top = ids_ref.shape[0]
     tiles = model // LANES
-    parts = send_sems.shape[0]
-    per_part = EXPERTS // parts
-    part_rows = per_part * tiles * CAP
-
     _, _, gate = router_gates(logits_ref[...])
     gate = gate.astype(bf16).astype(f32)
     ids = jnp.transpose(ids_ref[...])
@@ -75,18 +70,12 @@
         weight = jnp.where(hit, gates[:, n : n + 1], weight)
     row_i = lax.broadcasted_iota(jnp.int32, (tokens, tokens), 0)
     col_i = lax.broadcasted_iota(jnp.int32, (tokens, tokens), 1)
-    before = jnp.dot(
-        (col_i < row_i).astype(bf16), named.astype(bf16), preferred_element_type=f32
-    )
+    before = jnp.dot((col_i < row_i).astype(bf16), named.astype(bf16), preferred_element_type=f32)
     token = lax.broadcasted_iota(jnp.int32, (tokens, EXPERTS), 0).astype(f32)
     for s in range(CAP):
         here = jnp.where((before == float(s)) & (named > 0.0), 1.0, 0.0)
         table_ref[s : s + 1, :] = jnp.sum(here * token, axis=0, keepdims=True).astype(jnp.int32)
         gates_ref[s : s + 1, :] = jnp.sum(here * weight, axis=0, keepdims=True)
-    table_copy = pltpu.make_async_copy(table_ref, table_smem, sems.at[0])
-    gates_copy = pltpu.make_async_copy(gates_ref, gates_smem, sems.at[1])
-    table_copy.start()
-    gates_copy.start()
     slots = []
     for n in range(top):
         hit = ids[:, n : n + 1] == expert
@@ -95,22 +84,45 @@
     coefficient = coefficient_row(ratio_ref, lengths_ref, chosen_ref)
     lane = lax.broadcasted_iota(jnp.int32, (tokens, coefficient.shape[1]), 1)
     row = lax.broadcasted_iota(jnp.int32, (tokens, coefficient.shape[1]), 0)
-    own = jnp.sum(
-        jnp.where(lane == row + start_ref[0], coefficient, 0.0), axis=1, keepdims=True
-    )
+    own = jnp.sum(jnp.where(lane == row + start_ref[0], coefficient, 0.0), axis=1, keepdims=True)
     for tile in range(tiles):
         cot = cot_ref[:, tile * LANES : (tile + 1) * LANES].astype(f32)
         rows_ref[pl.ds(tile, tokens, stride=tiles), :] = (own * cot).astype(bf16).astype(f32)
-    table_copy.wait()
-    gates_copy.wait()
+
+
+def plan_send(lengths, chosen, start, ratio, ids, logits, cot):
+    tokens, model = cot.shape
+    smem = pl.BlockSpec(memory_space=pltpu.SMEM)
+    vmem = pl.BlockSpec(memory_space=pltpu.VMEM)
+    return pl.pallas_call(
+        plan_kernel,
+        in_specs=[smem, smem, smem, vmem, vmem, vmem, vmem],
+        out_specs=[vmem, vmem, vmem, vmem],
+        out_shape=[
+            jax.ShapeDtypeStruct((tokens * (model // LANES), LANES), f32),
+            jax.ShapeDtypeStruct(ids.shape, jnp.int32),
+            jax.ShapeDtypeStruct((CAP, EXPERTS), jnp.int32),
+            jax.ShapeDtypeStruct((CAP, EXPERTS), f32),
+        ],
+        compiler_params=pltpu.CompilerParams(vmem_limit_bytes=VMEM),
+        cost_estimate=pl.CostEstimate(flops=0, bytes_accessed=1_500_000, transcendentals=0),
+        name="plan_send",
+    )(lengths, chosen, start, ratio, ids, logits, cot)
+
+
+def send_kernel(table_ref, gates_ref, rows_ref, send_hbm, pair_ref, send_ref, send_sems):
+    tiles = pair_ref.shape[1] // CAP
+    parts = send_sems.shape[0]
+    per_part = EXPERTS // parts
+    part_rows = per_part * tiles * CAP
 
     def place(group, carry):
         for u in range(PLACED):
             e = group * PLACED + u
             for s in range(CAP):
-                token = table_smem[s, e]
+                token = table_ref[s, e]
                 block = rows_ref[pl.ds(pl.multiple_of(token * tiles, 8), tiles), :]
-                pair_ref[u, pl.ds(s, tiles, stride=CAP), :] = block * gates_smem[s, e]
+                pair_ref[u, pl.ds(s, tiles, stride=CAP), :] = block * gates_ref[s, e]
         for u in range(PLACED):
             at = pl.multiple_of((group * PLACED + u) * (tiles * CAP), 16)
             send_ref[pl.ds(at, tiles * CAP), :] = pair_ref[u].astype(bf16)
@@ -131,41 +143,31 @@
         send_copy(part).wait()
 
 
-def build_send(lengths, chosen, start, ratio, ids, logits, cot):
-    tokens, model = cot.shape
-    tiles = model // LANES
+def build_send(table, gates, token_rows, tokens):
+    tiles = token_rows.shape[0] // tokens
     rows = EXPERTS * CAP * tiles
     parts = 8
     smem = pl.BlockSpec(memory_space=pltpu.SMEM)
     vmem = pl.BlockSpec(memory_space=pltpu.VMEM)
     return pl.pallas_call(
         send_kernel,
-        in_specs=[smem, smem, smem, vmem, vmem, vmem, vmem],
-        out_specs=[pl.BlockSpec(memory_space=pl.ANY), vmem],
-        out_shape=[
-            jax.ShapeDtypeStruct((rows, LANES), bf16),
-            jax.ShapeDtypeStruct(ids.shape, jnp.int32),
-        ],
+        in_specs=[smem, smem, vmem],
+        out_specs=pl.BlockSpec(memory_space=pl.ANY),
+        out_shape=jax.ShapeDtypeStruct((rows, LANES), bf16),
         scratch_shapes=[
-            pltpu.VMEM((tokens * tiles, LANES), f32),
             pltpu.VMEM((PLACED, tiles * CAP, LANES), f32),
-            pltpu.VMEM((8, EXPERTS), jnp.int32),
-            pltpu.VMEM((8, EXPERTS), f32),
-            pltpu.SMEM((8, EXPERTS), jnp.int32),
-            pltpu.SMEM((8, EXPERTS), f32),
             pltpu.VMEM((rows, LANES), bf16),
-            pltpu.SemaphoreType.DMA((2,)),
             pltpu.SemaphoreType.DMA((parts,)),
         ],
         compiler_params=pltpu.CompilerParams(vmem_limit_bytes=VMEM),
         cost_estimate=pl.CostEstimate(flops=0, bytes_accessed=8_000_000, transcendentals=0),
         name="build_send",
-    )(lengths, chosen, start, ratio, ids, logits, cot)
+    )(table, gates, token_rows)
 
 
 def dot_kernel(got_hbm, saved_hbm, out_ref, rows_hbm, got_ref, saved_ref, acc_ref, sems):
-    sources, wide = out_ref.shape
-    per_owner = wide // 8
+    sources = out_ref.shape[0]
+    per_owner = EXPERTS // sources
     parts = sems.shape[1]
     rows = got_ref.shape[0] // parts
     owners = sources // parts
@@ -195,8 +197,9 @@
             product = got_ref[at, :].astype(f32) * saved_ref[at, :].astype(f32)
             acc_ref[p] = jnp.sum(product.reshape(tall // 8, 8, LANES), axis=0)
         product = acc_ref[...].reshape(owners, per_owner, 8, LANES)
+        spare = jnp.zeros((owners, LANES - 8 * per_owner), f32)
         out_ref[pl.ds(pl.multiple_of(part * owners, 8), owners), :] = jnp.concatenate(
-            [jnp.sum(product[:, e], axis=2) for e in range(per_owner)], axis=1
+            [jnp.sum(product[:, e], axis=2) for e in range(per_owner)] + [spare], axis=1
         )
         return carry
 
@@ -213,7 +216,7 @@
         in_specs=[anywhere, anywhere],
         out_specs=[pl.BlockSpec(memory_space=pltpu.VMEM), anywhere],
         out_shape=[
-            jax.ShapeDtypeStruct((sources, per_owner * 8), f32),
+            jax.ShapeDtypeStruct((sources, LANES), f32),
             jax.ShapeDtypeStruct(got.shape, got.dtype),
         ],
         scratch_shapes=[
@@ -230,8 +233,8 @@
 
 def router_kernel(terms_ref, ids_ref, slot_ref, logits_ref, out_ref):
     top, tokens = ids_ref.shape
-    owners, wide = terms_ref.shape
-    per_owner = wide // 8
+    owners = terms_ref.shape[0]
+    per_owner = EXPERTS // owners
     affinity, total, gate = router_gates(logits_ref[...])
     ids = jnp.transpose(ids_ref[...])
     slots = jnp.transpose(slot_ref[...])
@@ -438,12 +441,9 @@
     ]
 
 
-def gather_ring(latent, count):
+def gather_ring(rows, count):
     rings = count // 4
-    return jnp.concatenate(
-        [latent]
-        + [lax.ppermute(latent, "ctx", ctx_moves(count, 0, rings - d, 0)) for d in range(1, rings)]
-    )
+    return [lax.ppermute(rows, "ctx", ctx_moves(count, 0, rings - d, 0)) for d in range(1, rings)]
 
 
 def ctx_places(count):
@@ -468,28 +468,31 @@
     ]
 
 
-def reduce_over_ring(held, count):
+def ring_terms(held, count):
     low = held.astype(bf16)
-    mine = held[:, 0]
-    for d in range(1, count // 4):
-        mine = mine + lax.ppermute(low[:, d], "ctx", ctx_moves(count, 0, d, 0)).astype(f32)
-    return mine
+    return [held[:, 0]] + [
+        lax.ppermute(low[:, d], "ctx", ctx_moves(count, 0, d, 0)) for d in range(1, count // 4)
+    ]
 
 
 def reduce_answer(rows, count):
     return rows[0] + lax.ppermute(rows[1], "ctx", ctx_moves(count, 1, 0, 0))
 
 
-def reduce_prompt(rows, ctx_count, resp_count):
+def prompt_terms(rows, resp_count):
     rings = resp_count // 2
     me = lax.axis_index("resp")
     my_ring, my_far = me // 2, me % 2
     blocks = rows.reshape(2, rings, 2, rows.shape[1] // resp_count, rows.shape[2])
     twice = jnp.concatenate([blocks, blocks[:, : rings - 1]], axis=1)
     blocks = lax.dynamic_slice_in_dim(twice, my_ring, rings, axis=1)
-    mine = blocks[:, 0]
-    for d in range(1, rings):
-        mine = mine + lax.ppermute(blocks[:, d], "resp", resp_moves(resp_count, d, 0))
+    parts = [blocks[:, 0]] + [
+        lax.ppermute(blocks[:, d], "resp", resp_moves(resp_count, d, 0)) for d in range(1, rings)
+    ]
+    return parts, my_far
+
+
+def reduce_prompt_far(mine, my_far, ctx_count, resp_count):
     own = lax.dynamic_index_in_dim(mine, my_far, axis=1, keepdims=False)
     others = lax.dynamic_index_in_dim(mine, 1 - my_far, axis=1, keepdims=False)
     return (
@@ -523,11 +526,20 @@
     ids = expert_ids[0].T
     logits = router_logits[0].T
 
+    far_moves = ctx_moves(ctx_count, 1, 0, 0)
+    token_rows, slot, table, gates = plan_send(
+        lengths, chosen, start, log_ratio, ids, logits, moe_cot[0]
+    )
     ring = gather_ring(prompt_latent, ctx_count)
-    ring, cot = lax.optimization_barrier((ring, moe_cot[0]))
-    sent, slot = build_send(lengths, chosen, start, log_ratio, ids, logits, cot)
-    far = lax.ppermute(ring, "ctx", ctx_moves(ctx_count, 1, 0, 0))
-    sent, around = lax.optimization_barrier((sent, jnp.concatenate([ring, far])))
+    far = lax.ppermute(prompt_latent, "ctx", far_moves)
+    ring, far, token_rows, table, gates = lax.optimization_barrier(
+        (ring, far, token_rows, table, gates)
+    )
+    ring = jnp.concatenate(ring)
+    far_ring = lax.ppermute(ring, "ctx", far_moves)
+    sent = build_send(table, gates, token_rows, tokens)
+    sent, ring, far, far_ring = lax.optimization_barrier((sent, ring, far, far_ring))
+    around = jnp.concatenate([prompt_latent, ring, far, far_ring])
     other = lax.ppermute(around, "ctx", ctx_moves(ctx_count, 0, 0, 1))
     arrived = lax.all_to_all(
         unflat(sent, devices, per_owner, CAP, model), ("ctx", "resp"), 0, 0, tiled=True
@@ -538,17 +550,18 @@
         jnp.concatenate([around, other]), response_latent[0].T,
     )
     held = reduce_over_cores(keep, send, ctx_count)
+    around = ring_terms(held, ctx_count)
     terms, rows = slot_dots(flat(arrived), flat(expert_outputs), devices, per_owner)
-    mine = reduce_over_ring(held, ctx_count)
-    mine, terms = lax.optimization_barrier((mine, terms))
+    around, terms = lax.optimization_barrier((around, terms))
+    mine = sum(part.astype(f32) for part in around)
     returned = lax.all_to_all(terms, ("ctx", "resp"), 0, 0, tiled=True)
     prompt_rows = prompt_latent.shape[0]
     grad_response = reduce_answer(mine[:, prompt_rows:], ctx_count)[None]
-    grad_prompt = reduce_prompt(mine[:, :prompt_rows], ctx_count, resp_count)
-
-    returned, grad_prompt, grad_response = lax.optimization_barrier(
-        (returned, grad_prompt, grad_response)
-    )
+    parts, my_far = prompt_terms(mine[:, :prompt_rows], resp_count)
+    blocks = sum(parts)
+    returned, _ = lax.optimization_barrier((returned, blocks))
+    grad_prompt = reduce_prompt_far(blocks, my_far, ctx_count, resp_count)
+
     grad_router = router_grad(returned, ids, slot, logits)
     expert_row_grads = unflat(rows, devices, per_owner, CAP, model)
     return (grad_query[None], grad_prompt, grad_response, expert_row_grads, grad_router.T[None])

time: 165 us -> 154 us (0.933)
  waiting for transfers between devices: 62.6 us -> 55.7 us
  starting transfers between devices: 44.8 us -> 40.5 us
  other arithmetic: 5.64 us -> 3.44 us
    ppermute x13 -> x14, waiting for transfers between devices: 59.1 us -> 1.08 us  [the longest x1 1.05 us: on_device(): far_ring = lax.ppermute(ring, 'ctx', far_moves)]
    all_to_all x1, waiting for transfers between devices: 0.01 us -> 48.1 us  [on_device(): lax.all_to_all(unflat(sent, devices, per_owner, CAP, model), ('ctx', 'res...]
    ppermute x13 -> x14, starting transfers between devices: 22 us -> 17.4 us  [the longest x3 4.99 us: gather_ring(): lax.ppermute(rows, 'ctx', ctx_moves(count, 0, rings - d, 0))]
    all_to_all x1, waiting for transfers between devices: 0.01 us -> 3.16 us  [on_device(): returned = lax.all_to_all(terms, ('ctx', 'resp'), 0, 0, tiled=True)]
    concatenate x4 -> x2, other arithmetic: 2.34 us -> 0.13 us  [the longest x1 0.07 us: prompt_terms(): twice = jnp.concatenate([blocks, blocks[:, :rings - 1]], axis=1)]
    pallas_call x1 -> x2, Pallas kernels: 6.28 us -> 7.14 us  [the longest x1 4.51 us: build_send(): pl.pallas_call(send_kernel, in_specs=[smem, smem, vmem], out_specs=pl.Blo...]
  transfers between devices with their start and end apart: 18 -> 19, of which waited for: 8 -> 5; matrix products, arithmetic and copies ran while one was open for 3% -> 2% of each run, Pallas kernels for 22% -> 32%
where the time goes in v3:
time: 154 us; the launch traced here: 153 us
  waiting for transfers between devices  55.7 us (36%)
  Pallas kernels  49.1 us (32%)
  starting transfers between devices  40.5 us (26%)
  other arithmetic  3.44 us (2%)
  local copies, waits for them, and re-layouts  2.73 us (2%)
  between operations  1.57 us (1%)
    all_to_all x1, waiting for transfers between devices, on_device(): lax.all_to_all(unflat(sent, devices, per_owner, CAP, model), ('ctx', 'res...  48.1 us
    pallas_call x1, Pallas kernels, attention(): pl.pallas_call(attention_kernel, grid=(steps,), in_specs=[smem, smem, sme...  30.6 us
    all_to_all x1, starting transfers between devices, on_device(): lax.all_to_all(unflat(sent, devices, per_owner, CAP, model), ('ctx', 'res...  11.7 us
    pallas_call x1, Pallas kernels, slot_dots(): pl.pallas_call(dot_kernel, in_specs=[anywhere, anywhere], out_specs=[pl.B...  9.11 us
    all_to_all x1, starting transfers between devices, on_device(): returned = lax.all_to_all(terms, ('ctx', 'resp'), 0, 0, tiled=True)  8.17 us
    ppermute x3, starting transfers between devices, gather_ring(): lax.ppermute(rows, 'ctx', ctx_moves(count, 0, rings - d, 0))  4.99 us
    pallas_call x1, Pallas kernels, build_send(): pl.pallas_call(send_kernel, in_specs=[smem, smem, vmem], out_specs=pl.Blo...  4.51 us
    ppermute x1, starting transfers between devices, reduce_prompt_far(): lax.ppermute(others[0], 'resp', resp_moves(resp_count, 0, 1))  3.21 us
  transfers between devices with their start and end apart: 19, of which 5 were waited for; matrix products, arithmetic and copies ran while one was open for 2% of the time, Pallas kernels for 32%

profile of v3, /device:TPU:1, one launch (start us, length us, event | category | flops | bytes accessed | tf_op | source)
XLA Modules:
  0.0 153.1 jit_solution(16116842409993293515)
XLA Ops:
  0.6 2.5 %collective-permute-start.3 = (bf16[64,576]{1,0:T(8,128)(2,1)}, bf16[64,576]{1,0:T(8,128)(2,1)S(1)}, u32[]{:S(2)}, u32[]{:S(2)}) collective-permute-start(bf16[64,576]{1,0:T(8,128)(2,1)} %param.13), channel_id=1, source_target_pairs={{0,64},{8,72},{16,80},{24,88},{32,96},{40,104},{48,112},{56,120},{... | collective-permute-start | bytes 221192 | tf_op jit(solution)/shard_map/ppermute | solution.py:534
  3.2 1.3 collective-permute-start.2
  4.5 2.6 %collective-permute-start.1 = (bf16[64,576]{1,0:T(8,128)(2,1)}, bf16[64,576]{1,0:T(8,128)(2,1)S(1)}, u32[]{:S(2)}, u32[]{:S(2)}) collective-permute-start(bf16[64,576]{1,0:T(8,128)(2,1)} %param.13), channel_id=1, source_target_pairs={{0,32},{8,40},{16,48},{24,56},{32,0},{40,8},{48,16},{56,24},{64,96... | collective-permute-start | bytes 221192 | tf_op jit(solution)/shard_map/ppermute | solution.py:446
  7.1 1.1 collective-permute-start
  8.8 2.6 %plan_send.1 = (f32[1792,128]{1,0:T(8,128)}, s32[8,32]{1,0:T(8,128)}, s32[2,256]{1,0:T(2,128)}, f32[2,256]{1,0:T(2,128)}) custom-call(s32[1,2]{1,0:T(1,128)} %lengths_ref.3, s32[1]{0:T(128)S(6)} %copy.46.chosen_ref, s32[1]{0:T(128)} %bitcast.2.start_ref, f32[1,512]{1,0:T(1,128)} %ratio_ref.3, s32[8,32]{1,0:T(8,128)} %bitcast.97, f32[8,32]{1,0:T(8,128)} %bitcast.99, ...), custom_call_target="tpu_custom_call" | custom-call | bytes 1500000 | tf_op jit(solution)/shard_map/plan_send/pallas_call | solution.py:97
  11.5 0.0 collective-permute-done.3
  11.5 0.0 collective-permute-done.2
  11.5 0.0 collective-permute-done.1
  11.5 0.0 collective-permute-done
  11.5 0.2 collective-permute-start.4
  11.7 4.5 %build_send.1 = bf16[28672,128]{1,0:T(8,128)(2,1)} custom-call(s32[2,256]{1,0:T(2,128)} %get-tuple-element.34.table_ref, f32[2,256]{1,0:T(2,128)} %get-tuple-element.35.gates_ref, f32[1792,128]{1,0:T(8,128)} %get-tuple-element.36.rows_ref), custom_call_target="tpu_custom_call" | custom-call | bytes 8000000 | tf_op jit(solution)/shard_map/build_send/pallas_call | solution.py:152
  16.2 1.0 collective-permute-done.4
  17.3 0.0 copy-start
  17.3 11.7 %all-to-all-start = ((bf16[128,2,2,7168]{3,2,1,0:T(2,128)(2,1)}), bf16[128,2,2,7168]{3,2,1,0:T(2,128)(2,1)}, u32[]{:S(2)}, u32[]{:S(2)}) async-start(bf16[128,2,2,7168]{3,2,1,0:T(2,128)(2,1)} %bitcast.89), calls=%async_computation | async-start | bytes 14680064 | tf_op jit(solution)/shard_map/all_to_all | solution.py:544
  29.0 0.0 copy-done
  29.0 0.1 pad_maximum_fusion
  29.1 0.2 copy.22
  29.3 1.2 collective-permute-start.5
  30.5 0.5 fusion.12.place_ref
  31.1 1.0 collective-permute-done.5
  32.1 0.3 copy.23
  32.4 0.1 constant_dynamic-update-slice_fusion.3.prompt_ref
  32.5 0.0 copy-start.2
  32.6 1.1 copy-done.2
  33.7 30.6 %attention.1 = (bf16[512,2304]{1,0:T(8,128)(2,1)}, bf16[8,96,576]{2,1,0:T(8,128)(2,1)}, bf16[8,96,576]{2,1,0:T(8,128)(2,1)}) custom-call(s32[1,2]{1,0:T(1,128)} %lengths_ref.3, s32[1]{0:T(128)S(6)} %copy.46.chosen_ref, s32[16]{0:T(128)} %fusion.12.place_ref, f32[1,512]{1,0:T(1,128)} %ratio_ref.3, bf16[512,2304]{1,0:T(8,128)(2,1)} %bitcast.103, ...), custom_call_target="tpu_custom_call" | custom-call | flops 16999999488 | bytes 9000000 | tf_op jit(solution)/shard_map/attention/pallas_call | solution.py:382
  64.3 0.4 collective-permute-start.6
  64.8 2.4 %collective-permute-done.6 = bf16[8,96,576]{2,1,0:T(8,128)(2,1)S(1)} collective-permute-done((bf16[8,96,576]{2,1,0:T(8,128)(2,1)}, bf16[8,96,576]{2,1,0:T(8,128)(2,1)S(1)}, u32[]{:S(2)}, u32[]{:S(2)}) %collective-permute-start.6) | collective-permute-done | bytes 884768 | tf_op jit(solution)/shard_map/ppermute | solution.py:459
  67.2 1.4 convert_add_fusion
  68.6 0.1 slice_bitcast_fusion.1
  68.7 2.0 %collective-permute-start.9 = (bf16[2,96,576]{2,1,0:T(8,128)(2,1)S(1)}, bf16[2,96,576]{2,1,0:T(8,128)(2,1)S(1)}, u32[]{:S(2)}, u32[]{:S(2)}) collective-permute-start(bf16[2,96,576]{2,1,0:T(8,128)(2,1)S(1)} %get-tuple-element.57), channel_id=1, source_target_pairs={{0,48},{8,56},{16,0},{24,8},{32,16},{40,24},{48,32},{56,40},{64,11... | collective-permute-start | bytes 663560 | tf_op jit(solution)/shard_map/ppermute | solution.py:474
  70.6 0.5 collective-permute-start.8
  71.2 0.6 collective-permute-start.7
  71.8 48.1 %all-to-all-done = bf16[128,2,2,7168]{3,2,1,0:T(2,128)(2,1)} async-done(((bf16[128,2,2,7168]{3,2,1,0:T(2,128)(2,1)}), bf16[128,2,2,7168]{3,2,1,0:T(2,128)(2,1)}, u32[]{:S(2)}, u32[]{:S(2)}) %all-to-all-start) | async-done | bytes 7340064 | tf_op jit(solution)/shard_map/all_to_all | solution.py:544
  119.8 9.1 %slot_dots.1 = (f32[128,128]{1,0:T(8,128)}, bf16[28672,128]{1,0:T(8,128)(2,1)}) custom-call(bf16[28672,128]{1,0:T(8,128)(2,1)} %bitcast.21.got_hbm, bf16[28672,128]{1,0:T(8,128)(2,1)} %bitcast.90), custom_call_target="tpu_custom_call" | custom-call | flops 8000000 | bytes 15000000 | tf_op jit(solution)/shard_map/slot_dots/pallas_call | solution.py:214
  129.0 0.0 collective-permute-done.9
  129.0 0.0 collective-permute-done.8
  129.0 0.0 collective-permute-done.7
  129.0 0.1 convert_add_fusion.1
  129.2 0.1 fusion
  129.3 0.1 collective-permute-start.10
  129.4 0.1 collective-permute-start.11
  129.5 2.6 %collective-permute-start.12 = (f32[2,2,8,576]{3,2,1,0:T(8,128)S(1)}, f32[2,2,8,576]{3,2,1,0:T(8,128)S(1)}, u32[]{:S(2)}, u32[]{:S(2)}) collective-permute-start(f32[2,2,8,576]{3,2,1,0:T(8,128)S(1)} %get-tuple-element.62), channel_id=1, source_target_pairs={{0,6},{1,7},{2,0},{3,1},{4,2},{5,3},{6,4},{7,5},{8,14},{9,15},{10,... | collective-permute-start | bytes 221192 | tf_op jit(solution)/shard_map/ppermute | solution.py:490
  132.1 8.2 %all-to-all-start.1 = ((f32[128,1,128]{2,1,0:T(1,128)}), f32[128,1,128]{2,1,0:T(1,128)S(1)}, u32[]{:S(2)}, u32[]{:S(2)}) async-start(f32[128,1,128]{2,1,0:T(1,128)} %bitcast.41), calls=%async_computation.1 | async-start | bytes 131072 | tf_op jit(solution)/shard_map/all_to_all | solution.py:557
  140.2 1.6 %collective-permute-start.16 = (f32[32,576]{1,0:T(8,128)S(1)}, f32[32,576]{1,0:T(8,128)S(1)}, u32[]{:S(2)}, u32[]{:S(2)}) collective-permute-start(f32[32,576]{1,0:T(8,128)S(1)} %slice_bitcast_fusion.4), channel_id=1, source_target_pairs={{0,64},{8,72},{16,80},{24,88},{32,96},{40,104},{48,112},{56,120},{... | collective-permute-start | bytes 221192 | tf_op jit(solution)/shard_map/ppermute | solution.py:479
  141.8 0.0 collective-permute-done.10
  141.8 0.0 collective-permute-done.11
  141.8 0.0 collective-permute-done.12
  141.9 0.1 collective-permute-start.13
  142.0 3.2 %collective-permute-start.14 = (f32[8,576]{1,0:T(8,128)S(1)}, f32[8,576]{1,0:T(8,128)S(1)}, u32[]{:S(2)}, u32[]{:S(2)}) collective-permute-start(f32[8,576]{1,0:T(8,128)S(1)} %get-tuple-element.64), channel_id=1, source_target_pairs={{0,1},{1,0},{2,3},{3,2},{4,5},{5,4},{6,7},{7,6},{8,9},{9,8},{10,11... | collective-permute-start | bytes 55304 | tf_op jit(solution)/shard_map/ppermute | solution.py:501
  145.2 0.6 collective-permute-start.15
  145.8 0.0 collective-permute-done.16
  145.8 0.6 fusion.2
  146.5 3.2 %all-to-all-done.1 = f32[128,1,128]{2,1,0:T(1,128)S(1)} async-done(((f32[128,1,128]{2,1,0:T(1,128)}), f32[128,1,128]{2,1,0:T(1,128)S(1)}, u32[]{:S(2)}, u32[]{:S(2)}) %all-to-all-start.1) | async-done | bytes 65568 | tf_op jit(solution)/shard_map/all_to_all | solution.py:557
  149.6 0.0 copy-start.1
  149.6 0.6 copy-done.1
  150.2 2.3 %router_grad.1 = f32[8,32]{1,0:T(8,128)} custom-call(f32[128,128]{1,0:T(8,128)} %bitcast.96, s32[8,32]{1,0:T(8,128)} %bitcast.98, s32[8,32]{1,0:T(8,128)} %get-tuple-element.56.slot_ref, f32[8,32]{1,0:T(8,128)} %bitcast.100), custom_call_target="tpu_custom_call" | custom-call | tf_op jit(solution)/shard_map/router_grad/pallas_call | solution.py:262
  152.5 0.0 collective-permute-done.13
  152.5 0.0 collective-permute-done.14
  152.5 0.0 collective-permute-done.15
  152.5 0.6 fusion.8
  (15 shorter events, 0.3 us)
Async XLA Ops:
  0.6 10.8 %collective-permute-start.3 = (bf16[64,576]{1,0:T(8,128)(2,1)}, bf16[64,576]{1,0:T(8,128)(2,1)S(1)}, u32[]{:S(2)}, u32[]{:S(2)}) collective-permute-start(bf16[64,576]{1,0:T(8,128)(2,1)} %param.13), channel_id=1, source_target_pairs={{0,64},{8,72},{16,80},{24,88},{32,96},{40,104},{48,112},{56,120},{... | collective-permute-start | bytes 221192 | tf_op jit(solution)/shard_map/ppermute | solution.py:534
  3.2 8.3 %collective-permute-start.2 = (bf16[64,576]{1,0:T(8,128)(2,1)}, bf16[64,576]{1,0:T(8,128)(2,1)S(1)}, u32[]{:S(2)}, u32[]{:S(2)}) collective-permute-start(bf16[64,576]{1,0:T(8,128)(2,1)} %param.13), channel_id=1, source_target_pairs={{0,16},{8,24},{16,32},{24,40},{32,48},{40,56},{48,0},{56,8},{64,80... | collective-permute-start | bytes 221192 | tf_op jit(solution)/shard_map/ppermute | solution.py:446
  4.5 7.0 %collective-permute-start.1 = (bf16[64,576]{1,0:T(8,128)(2,1)}, bf16[64,576]{1,0:T(8,128)(2,1)S(1)}, u32[]{:S(2)}, u32[]{:S(2)}) collective-permute-start(bf16[64,576]{1,0:T(8,128)(2,1)} %param.13), channel_id=1, source_target_pairs={{0,32},{8,40},{16,48},{24,56},{32,0},{40,8},{48,16},{56,24},{64,96... | collective-permute-start | bytes 221192 | tf_op jit(solution)/shard_map/ppermute | solution.py:446
  7.1 4.4 %collective-permute-start = (bf16[64,576]{1,0:T(8,128)(2,1)}, bf16[64,576]{1,0:T(8,128)(2,1)S(1)}, u32[]{:S(2)}, u32[]{:S(2)}) collective-permute-start(bf16[64,576]{1,0:T(8,128)(2,1)} %param.13), channel_id=1, source_target_pairs={{0,48},{8,56},{16,0},{24,8},{32,16},{40,24},{48,32},{56,40},{64,11... | collective-permute-start | bytes 221192 | tf_op jit(solution)/shard_map/ppermute | solution.py:446
  11.5 5.7 %collective-permute-start.4 = (bf16[192,576]{1,0:T(8,128)(2,1)S(1)}, bf16[192,576]{1,0:T(8,128)(2,1)S(1)}, u32[]{:S(2)}, u32[]{:S(2)}) collective-permute-start(bf16[192,576]{1,0:T(8,128)(2,1)S(1)} %constant_dynamic-update-slice_fusion), channel_id=1, source_target_pairs={{0,64},{8,72},{16,80},{24,88},{32,96},{40,104},{48,112},{56,120},{... | collective-permute-start | bytes 663560 | tf_op jit(solution)/shard_map/ppermute | solution.py:539
  17.3 11.7 %copy-start = (bf16[64,576]{1,0:T(8,128)(2,1)S(1)}, bf16[64,576]{1,0:T(8,128)(2,1)}, u32[]{:S(2)}) copy-start(bf16[64,576]{1,0:T(8,128)(2,1)} %param.13) | copy-start | bytes 221188
  17.3 102.6 %all-to-all-start = ((bf16[128,2,2,7168]{3,2,1,0:T(2,128)(2,1)}), bf16[128,2,2,7168]{3,2,1,0:T(2,128)(2,1)}, u32[]{:S(2)}, u32[]{:S(2)}) async-start(bf16[128,2,2,7168]{3,2,1,0:T(2,128)(2,1)} %bitcast.89), calls=%async_computation | async-start | bytes 14680064 | tf_op jit(solution)/shard_map/all_to_all | solution.py:544
  29.3 2.8 %collective-permute-start.5 = (bf16[512,576]{0,1:T(8,128)(2,1)S(1)}, bf16[512,576]{0,1:T(8,128)(2,1)S(1)}, u32[]{:S(2)}, u32[]{:S(2)}) collective-permute-start(bf16[512,576]{0,1:T(8,128)(2,1)S(1)} %copy.22), channel_id=1, source_target_pairs={{0,8},{8,0},{16,24},{24,16},{32,40},{40,32},{48,56},{56,48},{64,72... | collective-permute-start | bytes 1769480 | tf_op jit(solution)/shard_map/ppermute | solution.py:543
  32.5 1.2 copy-start.2
  64.3 2.9 %collective-permute-start.6 = (bf16[8,96,576]{2,1,0:T(8,128)(2,1)}, bf16[8,96,576]{2,1,0:T(8,128)(2,1)S(1)}, u32[]{:S(2)}, u32[]{:S(2)}) collective-permute-start(bf16[8,96,576]{2,1,0:T(8,128)(2,1)} %get-tuple-element.46), channel_id=1, source_target_pairs={{0,8},{8,0},{16,24},{24,16},{32,40},{40,32},{48,56},{56,48},{64,72... | collective-permute-start | bytes 2654216 | tf_op jit(solution)/shard_map/ppermute | solution.py:459
  68.7 60.3 %collective-permute-start.9 = (bf16[2,96,576]{2,1,0:T(8,128)(2,1)S(1)}, bf16[2,96,576]{2,1,0:T(8,128)(2,1)S(1)}, u32[]{:S(2)}, u32[]{:S(2)}) collective-permute-start(bf16[2,96,576]{2,1,0:T(8,128)(2,1)S(1)} %get-tuple-element.57), channel_id=1, source_target_pairs={{0,48},{8,56},{16,0},{24,8},{32,16},{40,24},{48,32},{56,40},{64,11... | collective-permute-start | bytes 663560 | tf_op jit(solution)/shard_map/ppermute | solution.py:474
  70.6 58.4 %collective-permute-start.8 = (bf16[2,96,576]{2,1,0:T(8,128)(2,1)S(1)}, bf16[2,96,576]{2,1,0:T(8,128)(2,1)S(1)}, u32[]{:S(2)}, u32[]{:S(2)}) collective-permute-start(bf16[2,96,576]{2,1,0:T(8,128)(2,1)S(1)} %get-tuple-element.58), channel_id=1, source_target_pairs={{0,32},{8,40},{16,48},{24,56},{32,0},{40,8},{48,16},{56,24},{64,96... | collective-permute-start | bytes 663560 | tf_op jit(solution)/shard_map/ppermute | solution.py:474
  71.2 57.8 %collective-permute-start.7 = (bf16[2,96,576]{2,1,0:T(8,128)(2,1)S(1)}, bf16[2,96,576]{2,1,0:T(8,128)(2,1)S(1)}, u32[]{:S(2)}, u32[]{:S(2)}) collective-permute-start(bf16[2,96,576]{2,1,0:T(8,128)(2,1)S(1)} %get-tuple-element.59), channel_id=1, source_target_pairs={{0,16},{8,24},{16,32},{24,40},{32,48},{40,56},{48,0},{56,8},{64,80... | collective-permute-start | bytes 663560 | tf_op jit(solution)/shard_map/ppermute | solution.py:474
  129.3 12.5 %collective-permute-start.10 = (f32[2,2,8,576]{3,2,1,0:T(8,128)S(1)}, f32[2,2,8,576]{3,2,1,0:T(8,128)S(1)}, u32[]{:S(2)}, u32[]{:S(2)}) collective-permute-start(f32[2,2,8,576]{3,2,1,0:T(8,128)S(1)} %get-tuple-element.60), channel_id=1, source_target_pairs={{0,2},{1,3},{2,4},{3,5},{4,6},{5,7},{6,0},{7,1},{8,10},{9,11},{10,... | collective-permute-start | bytes 221192 | tf_op jit(solution)/shard_map/ppermute | solution.py:490
  129.4 12.4 %collective-permute-start.11 = (f32[2,2,8,576]{3,2,1,0:T(8,128)S(1)}, f32[2,2,8,576]{3,2,1,0:T(8,128)S(1)}, u32[]{:S(2)}, u32[]{:S(2)}) collective-permute-start(f32[2,2,8,576]{3,2,1,0:T(8,128)S(1)} %get-tuple-element.61), channel_id=1, source_target_pairs={{0,4},{1,5},{2,6},{3,7},{4,0},{5,1},{6,2},{7,3},{8,12},{9,13},{10,... | collective-permute-start | bytes 221192 | tf_op jit(solution)/shard_map/ppermute | solution.py:490
  129.5 12.4 %collective-permute-start.12 = (f32[2,2,8,576]{3,2,1,0:T(8,128)S(1)}, f32[2,2,8,576]{3,2,1,0:T(8,128)S(1)}, u32[]{:S(2)}, u32[]{:S(2)}) collective-permute-start(f32[2,2,8,576]{3,2,1,0:T(8,128)S(1)} %get-tuple-element.62), channel_id=1, source_target_pairs={{0,6},{1,7},{2,0},{3,1},{4,2},{5,3},{6,4},{7,5},{8,14},{9,15},{10,... | collective-permute-start | bytes 221192 | tf_op jit(solution)/shard_map/ppermute | solution.py:490
  132.1 17.6 %all-to-all-start.1 = ((f32[128,1,128]{2,1,0:T(1,128)}), f32[128,1,128]{2,1,0:T(1,128)S(1)}, u32[]{:S(2)}, u32[]{:S(2)}) async-start(f32[128,1,128]{2,1,0:T(1,128)} %bitcast.41), calls=%async_computation.1 | async-start | bytes 131072 | tf_op jit(solution)/shard_map/all_to_all | solution.py:557
  140.2 5.6 %collective-permute-start.16 = (f32[32,576]{1,0:T(8,128)S(1)}, f32[32,576]{1,0:T(8,128)S(1)}, u32[]{:S(2)}, u32[]{:S(2)}) collective-permute-start(f32[32,576]{1,0:T(8,128)S(1)} %slice_bitcast_fusion.4), channel_id=1, source_target_pairs={{0,64},{8,72},{16,80},{24,88},{32,96},{40,104},{48,112},{56,120},{... | collective-permute-start | bytes 221192 | tf_op jit(solution)/shard_map/ppermute | solution.py:479
  141.9 10.6 %collective-permute-start.13 = (f32[8,576]{1,0:T(8,128)S(1)}, f32[8,576]{1,0:T(8,128)S(1)}, u32[]{:S(2)}, u32[]{:S(2)}) collective-permute-start(f32[8,576]{1,0:T(8,128)S(1)} %get-tuple-element.63), channel_id=1, source_target_pairs={{0,64},{8,72},{16,80},{24,88},{32,96},{40,104},{48,112},{56,120},{... | collective-permute-start | bytes 55304 | tf_op jit(solution)/shard_map/ppermute | solution.py:500
  142.0 10.5 %collective-permute-start.14 = (f32[8,576]{1,0:T(8,128)S(1)}, f32[8,576]{1,0:T(8,128)S(1)}, u32[]{:S(2)}, u32[]{:S(2)}) collective-permute-start(f32[8,576]{1,0:T(8,128)S(1)} %get-tuple-element.64), channel_id=1, source_target_pairs={{0,1},{1,0},{2,3},{3,2},{4,5},{5,4},{6,7},{7,6},{8,9},{9,8},{10,11... | collective-permute-start | bytes 55304 | tf_op jit(solution)/shard_map/ppermute | solution.py:501
  145.2 7.3 %collective-permute-start.15 = (f32[8,576]{1,0:T(8,128)S(1)}, f32[8,576]{1,0:T(8,128)S(1)}, u32[]{:S(2)}, u32[]{:S(2)}) collective-permute-start(f32[8,576]{1,0:T(8,128)S(1)} %get-tuple-element.65), channel_id=1, source_target_pairs={{0,65},{1,64},{2,67},{3,66},{4,69},{5,68},{6,71},{7,70},{8,73},{9,... | collective-permute-start | bytes 55304 | tf_op jit(solution)/shard_map/ppermute | solution.py:502
  149.6 0.6 copy-start.1

commit v4 on v3

--- a/solution.py
+++ b/solution.py
@@ -146,7 +146,7 @@
 def build_send(table, gates, token_rows, tokens):
     tiles = token_rows.shape[0] // tokens
     rows = EXPERTS * CAP * tiles
-    parts = 8
+    parts = 16
     smem = pl.BlockSpec(memory_space=pltpu.SMEM)
     vmem = pl.BlockSpec(memory_space=pltpu.VMEM)
     return pl.pallas_call(
@@ -209,7 +209,7 @@
 
 
 def slot_dots(got, saved, sources, per_owner):
-    parts = 8
+    parts = 16
     anywhere = pl.BlockSpec(memory_space=pl.ANY)
     return pl.pallas_call(
         dot_kernel,

time: 154 us -> 154 us (level)
  no operation moved by 1% of the time
where the time goes in v4:
time: 154 us; the launch traced here: 153 us
  waiting for transfers between devices  55.8 us (36%)
  Pallas kernels  49.1 us (32%)
  starting transfers between devices  40.5 us (26%)
  other arithmetic  3.44 us (2%)
  local copies, waits for them, and re-layouts  2.73 us (2%)
  between operations  1.57 us (1%)
    all_to_all x1, waiting for transfers between devices, on_device(): lax.all_to_all(unflat(sent, devices, per_owner, CAP, model), ('ctx', 'res...  48.1 us
    pallas_call x1, Pallas kernels, attention(): pl.pallas_call(attention_kernel, grid=(steps,), in_specs=[smem, smem, sme...  30.6 us
    all_to_all x1, starting transfers between devices, on_device(): lax.all_to_all(unflat(sent, devices, per_owner, CAP, model), ('ctx', 'res...  11.7 us
    pallas_call x1, Pallas kernels, slot_dots(): pl.pallas_call(dot_kernel, in_specs=[anywhere, anywhere], out_specs=[pl.B...  9.15 us
    all_to_all x1, starting transfers between devices, on_device(): returned = lax.all_to_all(terms, ('ctx', 'resp'), 0, 0, tiled=True)  8.13 us
    ppermute x3, starting transfers between devices, gather_ring(): lax.ppermute(rows, 'ctx', ctx_moves(count, 0, rings - d, 0))  4.99 us
    pallas_call x1, Pallas kernels, build_send(): pl.pallas_call(send_kernel, in_specs=[smem, smem, vmem], out_specs=pl.Blo...  4.43 us
    ppermute x1, starting transfers between devices, reduce_prompt_far(): lax.ppermute(others[0], 'resp', resp_moves(resp_count, 0, 1))  3.21 us
  transfers between devices with their start and end apart: 19, of which 5 were waited for; matrix products, arithmetic and copies ran while one was open for 2% of the time, Pallas kernels for 32%

profile of v4, /device:TPU:1, one launch (start us, length us, event | category | flops | bytes accessed | tf_op | source)
XLA Modules:
  0.0 153.1 jit_solution(1155973342104702106)
XLA Ops:
  0.6 2.5 %collective-permute-start.3 = (bf16[64,576]{1,0:T(8,128)(2,1)}, bf16[64,576]{1,0:T(8,128)(2,1)S(1)}, u32[]{:S(2)}, u32[]{:S(2)}) collective-permute-start(bf16[64,576]{1,0:T(8,128)(2,1)} %param.13), channel_id=1, source_target_pairs={{0,64},{8,72},{16,80},{24,88},{32,96},{40,104},{48,112},{56,120},{... | collective-permute-start | bytes 221192 | tf_op jit(solution)/shard_map/ppermute | solution.py:534
  3.2 1.3 collective-permute-start.2
  4.5 2.6 %collective-permute-start.1 = (bf16[64,576]{1,0:T(8,128)(2,1)}, bf16[64,576]{1,0:T(8,128)(2,1)S(1)}, u32[]{:S(2)}, u32[]{:S(2)}) collective-permute-start(bf16[64,576]{1,0:T(8,128)(2,1)} %param.13), channel_id=1, source_target_pairs={{0,32},{8,40},{16,48},{24,56},{32,0},{40,8},{48,16},{56,24},{64,96... | collective-permute-start | bytes 221192 | tf_op jit(solution)/shard_map/ppermute | solution.py:446
  7.1 1.1 collective-permute-start
  8.8 2.6 %plan_send.1 = (f32[1792,128]{1,0:T(8,128)}, s32[8,32]{1,0:T(8,128)}, s32[2,256]{1,0:T(2,128)}, f32[2,256]{1,0:T(2,128)}) custom-call(s32[1,2]{1,0:T(1,128)} %lengths_ref.3, s32[1]{0:T(128)S(6)} %copy.46.chosen_ref, s32[1]{0:T(128)} %bitcast.2.start_ref, f32[1,512]{1,0:T(1,128)} %ratio_ref.3, s32[8,32]{1,0:T(8,128)} %bitcast.97, f32[8,32]{1,0:T(8,128)} %bitcast.99, ...), custom_call_target="tpu_custom_call" | custom-call | bytes 1500000 | tf_op jit(solution)/shard_map/plan_send/pallas_call | solution.py:97
  11.5 0.0 collective-permute-done.3
  11.5 0.0 collective-permute-done.2
  11.5 0.0 collective-permute-done.1
  11.5 0.0 collective-permute-done
  11.5 0.2 collective-permute-start.4
  11.7 4.4 %build_send.1 = bf16[28672,128]{1,0:T(8,128)(2,1)} custom-call(s32[2,256]{1,0:T(2,128)} %get-tuple-element.34.table_ref, f32[2,256]{1,0:T(2,128)} %get-tuple-element.35.gates_ref, f32[1792,128]{1,0:T(8,128)} %get-tuple-element.36.rows_ref), custom_call_target="tpu_custom_call" | custom-call | bytes 8000000 | tf_op jit(solution)/shard_map/build_send/pallas_call | solution.py:152
  16.1 1.1 collective-permute-done.4
  17.3 0.0 copy-start
  17.3 11.7 %all-to-all-start = ((bf16[128,2,2,7168]{3,2,1,0:T(2,128)(2,1)}), bf16[128,2,2,7168]{3,2,1,0:T(2,128)(2,1)}, u32[]{:S(2)}, u32[]{:S(2)}) async-start(bf16[128,2,2,7168]{3,2,1,0:T(2,128)(2,1)} %bitcast.89), calls=%async_computation | async-start | bytes 14680064 | tf_op jit(solution)/shard_map/all_to_all | solution.py:544
  29.0 0.0 copy-done
  29.0 0.1 pad_maximum_fusion
  29.1 0.2 copy.22
  29.3 1.2 collective-permute-start.5
  30.5 0.5 fusion.12.place_ref
  31.1 1.0 collective-permute-done.5
  32.1 0.3 copy.23
  32.4 0.1 constant_dynamic-update-slice_fusion.3.prompt_ref
  32.5 0.0 copy-start.2
  32.6 1.1 copy-done.2
  33.7 30.6 %attention.1 = (bf16[512,2304]{1,0:T(8,128)(2,1)}, bf16[8,96,576]{2,1,0:T(8,128)(2,1)}, bf16[8,96,576]{2,1,0:T(8,128)(2,1)}) custom-call(s32[1,2]{1,0:T(1,128)} %lengths_ref.3, s32[1]{0:T(128)S(6)} %copy.46.chosen_ref, s32[16]{0:T(128)} %fusion.12.place_ref, f32[1,512]{1,0:T(1,128)} %ratio_ref.3, bf16[512,2304]{1,0:T(8,128)(2,1)} %bitcast.103, ...), custom_call_target="tpu_custom_call" | custom-call | flops 16999999488 | bytes 9000000 | tf_op jit(solution)/shard_map/attention/pallas_call | solution.py:382
  64.3 0.4 collective-permute-start.6
  64.8 2.4 %collective-permute-done.6 = bf16[8,96,576]{2,1,0:T(8,128)(2,1)S(1)} collective-permute-done((bf16[8,96,576]{2,1,0:T(8,128)(2,1)}, bf16[8,96,576]{2,1,0:T(8,128)(2,1)S(1)}, u32[]{:S(2)}, u32[]{:S(2)}) %collective-permute-start.6) | collective-permute-done | bytes 884768 | tf_op jit(solution)/shard_map/ppermute | solution.py:459
  67.2 1.4 convert_add_fusion
  68.6 0.1 slice_bitcast_fusion.1
  68.7 2.0 %collective-permute-start.9 = (bf16[2,96,576]{2,1,0:T(8,128)(2,1)S(1)}, bf16[2,96,576]{2,1,0:T(8,128)(2,1)S(1)}, u32[]{:S(2)}, u32[]{:S(2)}) collective-permute-start(bf16[2,96,576]{2,1,0:T(8,128)(2,1)S(1)} %get-tuple-element.57), channel_id=1, source_target_pairs={{0,48},{8,56},{16,0},{24,8},{32,16},{40,24},{48,32},{56,40},{64,11... | collective-permute-start | bytes 663560 | tf_op jit(solution)/shard_map/ppermute | solution.py:474
  70.6 0.5 collective-permute-start.8
  71.2 0.6 collective-permute-start.7
  71.8 48.1 %all-to-all-done = bf16[128,2,2,7168]{3,2,1,0:T(2,128)(2,1)} async-done(((bf16[128,2,2,7168]{3,2,1,0:T(2,128)(2,1)}), bf16[128,2,2,7168]{3,2,1,0:T(2,128)(2,1)}, u32[]{:S(2)}, u32[]{:S(2)}) %all-to-all-start) | async-done | bytes 7340064 | tf_op jit(solution)/shard_map/all_to_all | solution.py:544
  119.8 9.2 %slot_dots.1 = (f32[128,128]{1,0:T(8,128)}, bf16[28672,128]{1,0:T(8,128)(2,1)}) custom-call(bf16[28672,128]{1,0:T(8,128)(2,1)} %bitcast.21.got_hbm, bf16[28672,128]{1,0:T(8,128)(2,1)} %bitcast.90), custom_call_target="tpu_custom_call" | custom-call | flops 8000000 | bytes 15000000 | tf_op jit(solution)/shard_map/slot_dots/pallas_call | solution.py:214
  129.0 0.0 collective-permute-done.9
  129.0 0.0 collective-permute-done.8
  129.0 0.0 collective-permute-done.7
  129.0 0.1 convert_add_fusion.1
  129.2 0.1 fusion
  129.3 0.1 collective-permute-start.10
  129.4 0.1 collective-permute-start.11
  129.5 2.6 %collective-permute-start.12 = (f32[2,2,8,576]{3,2,1,0:T(8,128)S(1)}, f32[2,2,8,576]{3,2,1,0:T(8,128)S(1)}, u32[]{:S(2)}, u32[]{:S(2)}) collective-permute-start(f32[2,2,8,576]{3,2,1,0:T(8,128)S(1)} %get-tuple-element.62), channel_id=1, source_target_pairs={{0,6},{1,7},{2,0},{3,1},{4,2},{5,3},{6,4},{7,5},{8,14},{9,15},{10,... | collective-permute-start | bytes 221192 | tf_op jit(solution)/shard_map/ppermute | solution.py:490
  132.1 8.1 %all-to-all-start.1 = ((f32[128,1,128]{2,1,0:T(1,128)}), f32[128,1,128]{2,1,0:T(1,128)S(1)}, u32[]{:S(2)}, u32[]{:S(2)}) async-start(f32[128,1,128]{2,1,0:T(1,128)} %bitcast.41), calls=%async_computation.1 | async-start | bytes 131072 | tf_op jit(solution)/shard_map/all_to_all | solution.py:557
  140.2 1.6 %collective-permute-start.16 = (f32[32,576]{1,0:T(8,128)S(1)}, f32[32,576]{1,0:T(8,128)S(1)}, u32[]{:S(2)}, u32[]{:S(2)}) collective-permute-start(f32[32,576]{1,0:T(8,128)S(1)} %slice_bitcast_fusion.4), channel_id=1, source_target_pairs={{0,64},{8,72},{16,80},{24,88},{32,96},{40,104},{48,112},{56,120},{... | collective-permute-start | bytes 221192 | tf_op jit(solution)/shard_map/ppermute | solution.py:479
  141.8 0.0 collective-permute-done.10
  141.8 0.0 collective-permute-done.11
  141.8 0.0 collective-permute-done.12
  141.9 0.1 collective-permute-start.13
  142.0 3.2 %collective-permute-start.14 = (f32[8,576]{1,0:T(8,128)S(1)}, f32[8,576]{1,0:T(8,128)S(1)}, u32[]{:S(2)}, u32[]{:S(2)}) collective-permute-start(f32[8,576]{1,0:T(8,128)S(1)} %get-tuple-element.64), channel_id=1, source_target_pairs={{0,1},{1,0},{2,3},{3,2},{4,5},{5,4},{6,7},{7,6},{8,9},{9,8},{10,11... | collective-permute-start | bytes 55304 | tf_op jit(solution)/shard_map/ppermute | solution.py:501
  145.2 0.6 collective-permute-start.15
  145.8 0.0 collective-permute-done.16
  145.8 0.6 fusion.2
  146.5 3.2 %all-to-all-done.1 = f32[128,1,128]{2,1,0:T(1,128)S(1)} async-done(((f32[128,1,128]{2,1,0:T(1,128)}), f32[128,1,128]{2,1,0:T(1,128)S(1)}, u32[]{:S(2)}, u32[]{:S(2)}) %all-to-all-start.1) | async-done | bytes 65568 | tf_op jit(solution)/shard_map/all_to_all | solution.py:557
  149.6 0.0 copy-start.1
  149.6 0.6 copy-done.1
  150.2 2.3 %router_grad.1 = f32[8,32]{1,0:T(8,128)} custom-call(f32[128,128]{1,0:T(8,128)} %bitcast.96, s32[8,32]{1,0:T(8,128)} %bitcast.98, s32[8,32]{1,0:T(8,128)} %get-tuple-element.56.slot_ref, f32[8,32]{1,0:T(8,128)} %bitcast.100), custom_call_target="tpu_custom_call" | custom-call | tf_op jit(solution)/shard_map/router_grad/pallas_call | solution.py:262
  152.5 0.0 collective-permute-done.13
  152.5 0.0 collective-permute-done.14
  152.5 0.0 collective-permute-done.15
  152.5 0.6 fusion.8
  (15 shorter events, 0.3 us)
Async XLA Ops:
  0.6 10.8 %collective-permute-start.3 = (bf16[64,576]{1,0:T(8,128)(2,1)}, bf16[64,576]{1,0:T(8,128)(2,1)S(1)}, u32[]{:S(2)}, u32[]{:S(2)}) collective-permute-start(bf16[64,576]{1,0:T(8,128)(2,1)} %param.13), channel_id=1, source_target_pairs={{0,64},{8,72},{16,80},{24,88},{32,96},{40,104},{48,112},{56,120},{... | collective-permute-start | bytes 221192 | tf_op jit(solution)/shard_map/ppermute | solution.py:534
  3.2 8.3 %collective-permute-start.2 = (bf16[64,576]{1,0:T(8,128)(2,1)}, bf16[64,576]{1,0:T(8,128)(2,1)S(1)}, u32[]{:S(2)}, u32[]{:S(2)}) collective-permute-start(bf16[64,576]{1,0:T(8,128)(2,1)} %param.13), channel_id=1, source_target_pairs={{0,16},{8,24},{16,32},{24,40},{32,48},{40,56},{48,0},{56,8},{64,80... | collective-permute-start | bytes 221192 | tf_op jit(solution)/shard_map/ppermute | solution.py:446
  4.5 7.0 %collective-permute-start.1 = (bf16[64,576]{1,0:T(8,128)(2,1)}, bf16[64,576]{1,0:T(8,128)(2,1)S(1)}, u32[]{:S(2)}, u32[]{:S(2)}) collective-permute-start(bf16[64,576]{1,0:T(8,128)(2,1)} %param.13), channel_id=1, source_target_pairs={{0,32},{8,40},{16,48},{24,56},{32,0},{40,8},{48,16},{56,24},{64,96... | collective-permute-start | bytes 221192 | tf_op jit(solution)/shard_map/ppermute | solution.py:446
  7.1 4.4 %collective-permute-start = (bf16[64,576]{1,0:T(8,128)(2,1)}, bf16[64,576]{1,0:T(8,128)(2,1)S(1)}, u32[]{:S(2)}, u32[]{:S(2)}) collective-permute-start(bf16[64,576]{1,0:T(8,128)(2,1)} %param.13), channel_id=1, source_target_pairs={{0,48},{8,56},{16,0},{24,8},{32,16},{40,24},{48,32},{56,40},{64,11... | collective-permute-start | bytes 221192 | tf_op jit(solution)/shard_map/ppermute | solution.py:446
  11.5 5.7 %collective-permute-start.4 = (bf16[192,576]{1,0:T(8,128)(2,1)S(1)}, bf16[192,576]{1,0:T(8,128)(2,1)S(1)}, u32[]{:S(2)}, u32[]{:S(2)}) collective-permute-start(bf16[192,576]{1,0:T(8,128)(2,1)S(1)} %constant_dynamic-update-slice_fusion), channel_id=1, source_target_pairs={{0,64},{8,72},{16,80},{24,88},{32,96},{40,104},{48,112},{56,120},{... | collective-permute-start | bytes 663560 | tf_op jit(solution)/shard_map/ppermute | solution.py:539
  17.3 11.7 %copy-start = (bf16[64,576]{1,0:T(8,128)(2,1)S(1)}, bf16[64,576]{1,0:T(8,128)(2,1)}, u32[]{:S(2)}) copy-start(bf16[64,576]{1,0:T(8,128)(2,1)} %param.13) | copy-start | bytes 221188
  17.3 102.6 %all-to-all-start = ((bf16[128,2,2,7168]{3,2,1,0:T(2,128)(2,1)}), bf16[128,2,2,7168]{3,2,1,0:T(2,128)(2,1)}, u32[]{:S(2)}, u32[]{:S(2)}) async-start(bf16[128,2,2,7168]{3,2,1,0:T(2,128)(2,1)} %bitcast.89), calls=%async_computation | async-start | bytes 14680064 | tf_op jit(solution)/shard_map/all_to_all | solution.py:544
  29.3 2.8 %collective-permute-start.5 = (bf16[512,576]{0,1:T(8,128)(2,1)S(1)}, bf16[512,576]{0,1:T(8,128)(2,1)S(1)}, u32[]{:S(2)}, u32[]{:S(2)}) collective-permute-start(bf16[512,576]{0,1:T(8,128)(2,1)S(1)} %copy.22), channel_id=1, source_target_pairs={{0,8},{8,0},{16,24},{24,16},{32,40},{40,32},{48,56},{56,48},{64,72... | collective-permute-start | bytes 1769480 | tf_op jit(solution)/shard_map/ppermute | solution.py:543
  32.5 1.2 copy-start.2
  64.3 2.9 %collective-permute-start.6 = (bf16[8,96,576]{2,1,0:T(8,128)(2,1)}, bf16[8,96,576]{2,1,0:T(8,128)(2,1)S(1)}, u32[]{:S(2)}, u32[]{:S(2)}) collective-permute-start(bf16[8,96,576]{2,1,0:T(8,128)(2,1)} %get-tuple-element.46), channel_id=1, source_target_pairs={{0,8},{8,0},{16,24},{24,16},{32,40},{40,32},{48,56},{56,48},{64,72... | collective-permute-start | bytes 2654216 | tf_op jit(solution)/shard_map/ppermute | solution.py:459
  68.7 60.3 %collective-permute-start.9 = (bf16[2,96,576]{2,1,0:T(8,128)(2,1)S(1)}, bf16[2,96,576]{2,1,0:T(8,128)(2,1)S(1)}, u32[]{:S(2)}, u32[]{:S(2)}) collective-permute-start(bf16[2,96,576]{2,1,0:T(8,128)(2,1)S(1)} %get-tuple-element.57), channel_id=1, source_target_pairs={{0,48},{8,56},{16,0},{24,8},{32,16},{40,24},{48,32},{56,40},{64,11... | collective-permute-start | bytes 663560 | tf_op jit(solution)/shard_map/ppermute | solution.py:474
  70.6 58.4 %collective-permute-start.8 = (bf16[2,96,576]{2,1,0:T(8,128)(2,1)S(1)}, bf16[2,96,576]{2,1,0:T(8,128)(2,1)S(1)}, u32[]{:S(2)}, u32[]{:S(2)}) collective-permute-start(bf16[2,96,576]{2,1,0:T(8,128)(2,1)S(1)} %get-tuple-element.58), channel_id=1, source_target_pairs={{0,32},{8,40},{16,48},{24,56},{32,0},{40,8},{48,16},{56,24},{64,96... | collective-permute-start | bytes 663560 | tf_op jit(solution)/shard_map/ppermute | solution.py:474
  71.2 57.9 %collective-permute-start.7 = (bf16[2,96,576]{2,1,0:T(8,128)(2,1)S(1)}, bf16[2,96,576]{2,1,0:T(8,128)(2,1)S(1)}, u32[]{:S(2)}, u32[]{:S(2)}) collective-permute-start(bf16[2,96,576]{2,1,0:T(8,128)(2,1)S(1)} %get-tuple-element.59), channel_id=1, source_target_pairs={{0,16},{8,24},{16,32},{24,40},{32,48},{40,56},{48,0},{56,8},{64,80... | collective-permute-start | bytes 663560 | tf_op jit(solution)/shard_map/ppermute | solution.py:474
  129.3 12.5 %collective-permute-start.10 = (f32[2,2,8,576]{3,2,1,0:T(8,128)S(1)}, f32[2,2,8,576]{3,2,1,0:T(8,128)S(1)}, u32[]{:S(2)}, u32[]{:S(2)}) collective-permute-start(f32[2,2,8,576]{3,2,1,0:T(8,128)S(1)} %get-tuple-element.60), channel_id=1, source_target_pairs={{0,2},{1,3},{2,4},{3,5},{4,6},{5,7},{6,0},{7,1},{8,10},{9,11},{10,... | collective-permute-start | bytes 221192 | tf_op jit(solution)/shard_map/ppermute | solution.py:490
  129.4 12.4 %collective-permute-start.11 = (f32[2,2,8,576]{3,2,1,0:T(8,128)S(1)}, f32[2,2,8,576]{3,2,1,0:T(8,128)S(1)}, u32[]{:S(2)}, u32[]{:S(2)}) collective-permute-start(f32[2,2,8,576]{3,2,1,0:T(8,128)S(1)} %get-tuple-element.61), channel_id=1, source_target_pairs={{0,4},{1,5},{2,6},{3,7},{4,0},{5,1},{6,2},{7,3},{8,12},{9,13},{10,... | collective-permute-start | bytes 221192 | tf_op jit(solution)/shard_map/ppermute | solution.py:490
  129.5 12.3 %collective-permute-start.12 = (f32[2,2,8,576]{3,2,1,0:T(8,128)S(1)}, f32[2,2,8,576]{3,2,1,0:T(8,128)S(1)}, u32[]{:S(2)}, u32[]{:S(2)}) collective-permute-start(f32[2,2,8,576]{3,2,1,0:T(8,128)S(1)} %get-tuple-element.62), channel_id=1, source_target_pairs={{0,6},{1,7},{2,0},{3,1},{4,2},{5,3},{6,4},{7,5},{8,14},{9,15},{10,... | collective-permute-start | bytes 221192 | tf_op jit(solution)/shard_map/ppermute | solution.py:490
  132.1 17.5 %all-to-all-start.1 = ((f32[128,1,128]{2,1,0:T(1,128)}), f32[128,1,128]{2,1,0:T(1,128)S(1)}, u32[]{:S(2)}, u32[]{:S(2)}) async-start(f32[128,1,128]{2,1,0:T(1,128)} %bitcast.41), calls=%async_computation.1 | async-start | bytes 131072 | tf_op jit(solution)/shard_map/all_to_all | solution.py:557
  140.2 5.6 %collective-permute-start.16 = (f32[32,576]{1,0:T(8,128)S(1)}, f32[32,576]{1,0:T(8,128)S(1)}, u32[]{:S(2)}, u32[]{:S(2)}) collective-permute-start(f32[32,576]{1,0:T(8,128)S(1)} %slice_bitcast_fusion.4), channel_id=1, source_target_pairs={{0,64},{8,72},{16,80},{24,88},{32,96},{40,104},{48,112},{56,120},{... | collective-permute-start | bytes 221192 | tf_op jit(solution)/shard_map/ppermute | solution.py:479
  141.9 10.6 %collective-permute-start.13 = (f32[8,576]{1,0:T(8,128)S(1)}, f32[8,576]{1,0:T(8,128)S(1)}, u32[]{:S(2)}, u32[]{:S(2)}) collective-permute-start(f32[8,576]{1,0:T(8,128)S(1)} %get-tuple-element.63), channel_id=1, source_target_pairs={{0,64},{8,72},{16,80},{24,88},{32,96},{40,104},{48,112},{56,120},{... | collective-permute-start | bytes 55304 | tf_op jit(solution)/shard_map/ppermute | solution.py:500
  142.0 10.5 %collective-permute-start.14 = (f32[8,576]{1,0:T(8,128)S(1)}, f32[8,576]{1,0:T(8,128)S(1)}, u32[]{:S(2)}, u32[]{:S(2)}) collective-permute-start(f32[8,576]{1,0:T(8,128)S(1)} %get-tuple-element.64), channel_id=1, source_target_pairs={{0,1},{1,0},{2,3},{3,2},{4,5},{5,4},{6,7},{7,6},{8,9},{9,8},{10,11... | collective-permute-start | bytes 55304 | tf_op jit(solution)/shard_map/ppermute | solution.py:501
  145.2 7.3 %collective-permute-start.15 = (f32[8,576]{1,0:T(8,128)S(1)}, f32[8,576]{1,0:T(8,128)S(1)}, u32[]{:S(2)}, u32[]{:S(2)}) collective-permute-start(f32[8,576]{1,0:T(8,128)S(1)} %get-tuple-element.65), channel_id=1, source_target_pairs={{0,65},{1,64},{2,67},{3,66},{4,69},{5,68},{6,71},{7,70},{8,73},{9,... | collective-permute-start | bytes 55304 | tf_op jit(solution)/shard_map/ppermute | solution.py:502
  149.6 0.6 copy-start.1
